TPU v7x, 32 devices: a whole 2x2x4 slice. The times are simulated.
32 devices in a mesh: pair: 2 (over y), dp: 16 (over z, x, core).
Axes of the slice: x: 2, y: 2, z: 4, core: 2. Of those that a mesh axis runs over, the one named last changes fastest.
Arguments:
- big_images: float32 [64, 3, 1024], P('dp'), may hold values from -3 to 3
- big_noise: float32 [64, 3, 1024], P('dp'), may hold values from -6 to 6
- small_images: float32 [32, 3, 256], P('dp'), may hold values from -3 to 3
- small_noise: float32 [32, 3, 256], P('dp'), may hold values from -6 to 6
- big_level: int32 [64], P('dp'), may hold values from 0 to 9
- small_level: int32 [32], P('dp'), may hold values from 0 to 9
- small_mask: int32 [32, 256], P('dp'), may hold values from 0 to 1
- owner_map: int32 [176], replicated, may hold values from 0 to 191, as said below
- blocks: float32 [192, 128, 128], P(('pair', 'dp')), may hold values from -0.375 to 0.375
- moments: float32 [192, 128, 128], P(('pair', 'dp')), may hold values from -0.0034179688 to 0.0034179688
- left_stats: float32 [192, 128, 128], P(('pair', 'dp')), as said below
- right_stats: float32 [192, 128, 128], P(('pair', 'dp')), as said below
- left_roots: float32 [192, 128, 128], P(('pair', 'dp')), as said below
- right_roots: float32 [192, 128, 128], P(('pair', 'dp')), as said below
- vectors: float32 [74, 256], replicated
- vec_first: float32 [74, 256], replicated, may hold values from -0.0012207031 to 0.0012207031
- vec_second: float32 [74, 256], replicated, as said below
Outputs:
- loss_sum: float32 [], replicated
- grad_norm: float32 [], replicated
- new_blocks: float32 [192, 128, 128], P(('pair', 'dp'))
- new_moments: float32 [192, 128, 128], P(('pair', 'dp'))
- new_left: float32 [192, 128, 128], P(('pair', 'dp'))
- new_right: float32 [192, 128, 128], P(('pair', 'dp'))
- new_vectors: float32 [74, 256], replicated
- new_vec_first: float32 [74, 256], replicated
- new_vec_second: float32 [74, 256], replicated
Inputs may be any that keep to these rules, and one draw needn't show every extreme that they name: `owner_map`: distinct slot numbers. `left_stats`: symmetric, positive diagonal. `right_stats`: symmetric, positive diagonal. `left_roots`: symmetric, positive diagonal. `right_roots`: symmetric, positive diagonal. `vec_second`: positive.
All inputs are finite; a program needn't handle non-finite values.
Results may differ from a plain program's by a relative error of at most 0.0053.
Values may be sent and summed in bfloat16 or wider, within the bound.
A program may use at most 320 MiB of HBM per device.

v0:
```python
from functools import partial
import math

import jax
import jax.numpy as jnp
from jax import lax
from jax.sharding import PartitionSpec as P

GROUPS = 32
SIDE = 32
SMALL_SIDE = 16
NSTEPS = 11
STEP = 10


HIGH = lax.Precision.HIGHEST
SIGMA_DATA = 0.5
SIGMA_MIN = 0.002
SIGMA_MAX = 80.0
RHO = 7.0
HUBER = 0.00054
CLIP = 1.0
BETA_ONE = 0.9
BETA_TWO = 0.999
DECAY = 0.0001
RATE_MATRIX = 0.02
RATE_VECTOR = 0.02
ROOT_HALF = 1.0 / math.sqrt(2.0)


def from_partner(value, axis, stride):
    mask = 2**stride
    pairs = [(source, source ^ mask) for source in range(lax.axis_size(axis))]
    return lax.ppermute(value, axis, pairs)


def product_plain(left, right):
    return jnp.dot(
        left.astype(jnp.bfloat16), right.astype(jnp.bfloat16), preferred_element_type=jnp.float32
    )


def product_keep(left, right):
    return (product_plain(left, right), (left.astype(jnp.bfloat16), right.astype(jnp.bfloat16)))


def product_pull(kept, grad):
    left, right = kept
    grad = grad.astype(jnp.bfloat16)
    left_grad = lax.dot_general(
        grad, right, (((1,), (1,)), ((), ())), preferred_element_type=jnp.float32
    )
    right_grad = lax.dot_general(
        left, grad, (((0,), (0,)), ((), ())), preferred_element_type=jnp.float32
    )
    return (left_grad, right_grad)


def product_low(left, right):
    rounded_product = jax.custom_vjp(product_plain)
    rounded_product.defvjp(product_keep, product_pull)
    return rounded_product(left, right)


def sigma_of(levels):
    lowest = SIGMA_MIN ** (1.0 / RHO)
    highest = SIGMA_MAX ** (1.0 / RHO)
    return (lowest + levels.astype(jnp.float32) / (NSTEPS - 1) * (highest - lowest)) ** RHO


def patches(values, side):
    grid = values.reshape(side, side, values.shape[-1])
    padded = jnp.pad(grid, ((1, 1), (1, 1), (0, 0)))
    taps = [
        padded[offset_y : offset_y + side, offset_x : offset_x + side]
        for offset_y in range(3)
        for offset_x in range(3)
    ]
    return jnp.concatenate(taps, axis=-1).reshape(side * side, -1)


def group_norm(values, groups):
    pixels, width = values.shape
    grouped = values.reshape(pixels, groups, width // groups)
    center = grouped - jnp.mean(grouped, axis=(0, 2), keepdims=True)
    spread = jnp.mean(center * center, axis=(0, 2), keepdims=True)
    return (center * lax.rsqrt(spread + 1e-06)).reshape(pixels, width)


def unpack_blocks(mats, width, block):

    def matrix(start, rows, cols):
        tall, broad = (rows // block, cols // block)
        part = mats[start : start + tall * broad]
        return (
            part.reshape(tall, broad, block, block).transpose(0, 2, 1, 3).reshape(rows, cols),
            start + tall * broad,
        )

    offset = 0
    convs = []
    for number in range(4):
        weight, offset = matrix(offset, 9 * width, width)
        convs.append(weight)
    times = []
    for number in range(2):
        weight, offset = matrix(offset, width, 2 * width)
        times.append(weight)
    triple, offset = matrix(offset, width, 3 * width)
    project, offset = matrix(offset, width, width)
    return (convs, times, triple, project)


def network(weights, vectors, noisy, sigma, side):
    convs, times, triple_weight, proj_weight = weights
    width = vectors.shape[1]
    half = width // 2
    freqs = jnp.exp(jnp.arange(half, dtype=jnp.float32) * (math.log(100.0) / (half - 1)))
    phase = jnp.log(sigma) / 4.0 * freqs
    embed = jnp.concatenate([jnp.sin(phase), jnp.cos(phase)])[None, :]
    scale_in = lax.rsqrt(sigma * sigma + SIGMA_DATA**2)
    hidden = jnp.dot(patches(noisy * scale_in, side), vectors[0:27], precision=HIGH) + vectors[27]
    for number in range(2):
        base = 28 + 6 * number
        active = jax.nn.silu(group_norm(hidden, GROUPS) * vectors[base] + vectors[base + 1])
        first = product_low(patches(active, side), convs[2 * number]) + vectors[base + 2]
        shifts = product_low(embed, times[number])[0]
        active = jax.nn.silu(
            group_norm(first, GROUPS) * (1.0 + shifts[:width] + vectors[base + 3])
            + shifts[width:]
            + vectors[base + 4]
        )
        second = product_low(patches(active, side), convs[2 * number + 1]) + vectors[base + 5]
        hidden = (hidden + second) * ROOT_HALF
    normed = group_norm(hidden, GROUPS) * vectors[40] + vectors[41]
    triple = product_low(normed, triple_weight)
    query = triple[:, :width] + vectors[42]
    keyset = triple[:, width : 2 * width]
    valueset = triple[:, 2 * width :] + vectors[43]
    scores = product_low(query, keyset.T) * (1.0 / math.sqrt(width))
    probs = jax.nn.softmax(scores, axis=-1)
    mixed = product_low(probs, valueset)
    hidden = (hidden + product_low(mixed, proj_weight) + vectors[44]) * ROOT_HALF
    active = jax.nn.silu(group_norm(hidden, GROUPS) * vectors[45] + vectors[46])
    head = vectors[47:74].reshape(9, 3, width).transpose(0, 2, 1).reshape(9 * width, 3)
    return jnp.dot(patches(active, side), head, precision=HIGH)


def consistency(weights, vectors, clean, noise, sigma, side):
    noisy = (clean + sigma * noise).T
    raw = network(weights, vectors, noisy, sigma, side)
    skip = SIGMA_DATA**2 / ((sigma - SIGMA_MIN) ** 2 + SIGMA_DATA**2)
    outer = (sigma - SIGMA_MIN) * SIGMA_DATA * lax.rsqrt(SIGMA_DATA**2 + sigma * sigma)
    return (skip * noisy + outer * raw).T


def pseudo_huber(student_out, target_out, mask_row, sigma_student, sigma_target):
    diff = student_out - target_out
    total = jnp.sum(mask_row[None, :] * diff * diff)
    bound = HUBER * math.sqrt(3 * diff.shape[1])
    return (jnp.sqrt(total + bound * bound) - bound) / (sigma_student - sigma_target)


def forward(mats, params, images, draws, sigmas, side):
    weights = unpack_blocks(mats, params.shape[1], mats.shape[1])

    def single(image, noise_one, sigma):
        return consistency(weights, params, image, noise_one, sigma, side)

    return jax.vmap(single)(images, draws, sigmas)


def group_loss(own, partner, mask, sigma_student, sigma_target):
    return jnp.sum(jax.vmap(pseudo_huber)(own, partner, mask, sigma_student, sigma_target))


def shampoo(grads, master, moments, left_stats, right_stats, left_roots, right_roots):
    first = BETA_ONE * moments + (1 - BETA_ONE) * grads
    left = BETA_TWO * left_stats + (1 - BETA_TWO) * jnp.einsum(
        "sij,skj->sik", grads, grads, precision=HIGH
    )
    right = BETA_TWO * right_stats + (1 - BETA_TWO) * jnp.einsum(
        "sji,sjk->sik", grads, grads, precision=HIGH
    )
    turned = jnp.einsum("sij,sjk->sik", left_roots, first, precision=HIGH)
    turned = jnp.einsum("sij,sjk->sik", turned, right_roots, precision=HIGH)
    norm_rms = jnp.sqrt(jnp.mean(turned * turned, axis=(1, 2), keepdims=True) + 1e-20)
    return (master - RATE_MATRIX * (turned / norm_rms + DECAY * master), first, left, right)


def adamw(grads, params, first, second):
    first = BETA_ONE * first + (1 - BETA_ONE) * grads
    second = BETA_TWO * second + (1 - BETA_TWO) * grads * grads
    fixed_first = first / (1 - BETA_ONE**STEP)
    fixed_second = second / (1 - BETA_TWO**STEP)
    return (
        params - RATE_VECTOR * (fixed_first / (jnp.sqrt(fixed_second) + 1e-08) + DECAY * params),
        first,
        second,
    )


def local(
    big_images,
    big_noise,
    small_images,
    small_noise,
    big_level,
    small_level,
    small_mask,
    owner_map,
    blocks,
    moments,
    left_stats,
    right_stats,
    left_roots,
    right_roots,
    vectors,
    vec_first,
    vec_second,
):
    slot_count = blocks.shape[0]
    whole = lax.all_gather(blocks.astype(jnp.bfloat16), ("pair", "dp"), axis=0, tiled=True)
    rounded = jnp.take(whole, owner_map, axis=0).astype(jnp.float32)
    pair_index = lax.axis_index("pair")
    groups = (
        (
            big_images,
            big_noise,
            big_level,
            jnp.ones((big_images.shape[0], SIDE * SIDE), jnp.float32),
            SIDE,
        ),
        (small_images, small_noise, small_level, small_mask.astype(jnp.float32), SMALL_SIDE),
    )
    mat_grad = jnp.zeros_like(rounded)
    vec_grad = jnp.zeros_like(vectors)
    loss_part = jnp.zeros((), jnp.float32)
    for clean, noise, level, mask, side in groups:
        sigma_target = sigma_of(level)
        sigma_student = sigma_of(level + 1)
        count = clean.shape[0] // 2
        start = pair_index * count
        other = (1 - pair_index) * count

        def take_half(values, begin, count=count):
            return lax.dynamic_slice_in_dim(values, begin, count, 0)

        images, draws = (take_half(clean, start), take_half(noise, start))
        low_sigma, high_sigma = (take_half(sigma_target, start), take_half(sigma_student, start))
        given = forward(
            rounded,
            vectors,
            take_half(clean, other),
            take_half(noise, other),
            take_half(sigma_target, other),
            side,
        )
        fixed = from_partner(given, "pair", 0)
        outputs, pull = jax.vjp(
            partial(forward, images=images, draws=draws, sigmas=high_sigma, side=side),
            rounded,
            vectors,
        )
        value, seed = jax.value_and_grad(group_loss)(
            outputs, fixed, take_half(mask, start), high_sigma, low_sigma
        )
        step_mats, step_vecs = pull(seed)
        mat_grad = mat_grad + step_mats
        vec_grad = vec_grad + step_vecs
        loss_part = loss_part + value
    flat = mat_grad.reshape(mat_grad.shape[0], -1)
    flat_total, vec_total, loss_total = lax.psum((flat, vec_grad, loss_part), ("pair", "dp"))
    slot_ids = lax.axis_index(("pair", "dp")) * slot_count + jnp.arange(slot_count, dtype=jnp.int32)
    selector = (slot_ids[:, None] == owner_map[None, :]).astype(jnp.float32)
    mine = jnp.dot(selector, flat_total, precision=HIGH)
    grad_norm = jnp.sqrt(jnp.sum(flat_total * flat_total) + jnp.sum(vec_total * vec_total))
    factor = jnp.minimum(1.0, CLIP / (grad_norm + 1e-06))
    slot_grad = mine.reshape(blocks.shape) * factor
    new_blocks, new_moments, new_left, new_right = shampoo(
        slot_grad, blocks, moments, left_stats, right_stats, left_roots, right_roots
    )
    new_vectors, new_first, new_second = adamw(vec_total * factor, vectors, vec_first, vec_second)
    return (
        loss_total,
        grad_norm,
        new_blocks,
        new_moments,
        new_left,
        new_right,
        new_vectors,
        new_first,
        new_second,
    )


def solution(mesh):
    placed = (
        P("dp", None, None),
        P("dp", None, None),
        P("dp", None, None),
        P("dp", None, None),
        P("dp"),
        P("dp"),
        P("dp", None),
        P(),
        P(("pair", "dp"), None, None),
        P(("pair", "dp"), None, None),
        P(("pair", "dp"), None, None),
        P(("pair", "dp"), None, None),
        P(("pair", "dp"), None, None),
        P(("pair", "dp"), None, None),
        P(),
        P(),
        P(),
    )
    return jax.shard_map(
        local,
        mesh=mesh,
        in_specs=placed,
        out_specs=(
            P(),
            P(),
            P(("pair", "dp"), None, None),
            P(("pair", "dp"), None, None),
            P(("pair", "dp"), None, None),
            P(("pair", "dp"), None, None),
            P(),
            P(),
            P(),
        ),
        check_vma=False,
    )
```

profile of v0, /device:TPU:0, one launch (start us, length us, event | category | flops | bytes accessed | tf_op | source)
XLA Modules:
  0.0 1278.5 jit_solution(27423968226011561)
XLA Ops:
  58.1 4.1 fusion.37
  75.6 12.7 copy.245
  98.7 10.7 gather_fusion
  123.1 15.9 %reshape.5842 = bf16[2304,256,1]{1,0,2:T(8,128)(2,1)} reshape(bf16[18,128,2,128]{3,2,1,0:T(2,128)(2,1)} %bitcast.1208) | data formatting | bytes 2359296 | tf_op jit(solution)/shard_map/jvp(vmap())/convert_element_type | solution.py:39
  139.0 7.9 add_reduce_fusion.3
  147.3 8.7 multiply_reduce_fusion.22
  159.7 3.8 fusion.36
  175.6 3.9 reshape.5843
  185.5 7.7 fusion.448
  202.1 4.0 fusion.449
  230.9 5.8 add_reduce_fusion.2
  245.3 4.2 multiply_reduce_fusion.20
  253.1 4.2 fusion.34
  281.8 4.3 reshape.5849
  292.3 7.6 fusion.451
  306.4 3.8 fusion.152
  380.7 7.2 broadcast_multiply_fusion
  389.7 4.2 slice_add_fusion.2
  395.0 4.6 broadcast_multiply_fusion.1
  399.6 8.3 fusion.470
  408.2 6.4 online-softmax
  422.4 6.4 online-softmax.1
  428.8 4.1 fusion.453
  439.0 5.7 pad_slice_fusion
  456.0 16.8 %fusion.120 = f32[2,3,1024]{2,1,0:T(4,128)} fusion(f32[2,1024,2304]{2,1,0:T(8,128)S(1)} %constant_dynamic-update-slice_fusion.73, f32[2304,3,1]{0,1,2:T(4,128)S(1)} %copy-done.154, f32[2]{0:T(128)S(1)} %copy-done.358, f32[2]{0:T(128)S(1)} %copy-done.362, f32[2,3,1024]{2,0,1:T(2,128)S(1)} %copy-done.175, f32[2]{0:T(128)S(1)} %copy-done.322, ...), kind=kOutput, calls=%fused_computation.281 | convolution fusion | flops 169900032 | bytes 18975768 | tf_op jit(solution)/shard_map/vmap()/dot_general | solution.py:146
  476.3 4.2 pad_slice_fusion.8
  530.0 3.9 reshape.5867
  533.9 4.0 reshape.5870
  537.9 3.9 reshape.5871
  543.4 12.6 copy.242
  556.0 12.7 copy.239
  568.7 12.8 copy.236
  587.3 19.1 %copy.255 = f32[2304,2,1024]{2,0,1:T(8,128)} copy(f32[2304,2,1024]{0,2,1:T(8,128)} %bitcast.409) | data formatting | bytes 37748736 | tf_op jit(solution)/shard_map/transpose(jvp(vmap()))/dot_general | solution.py:146
  606.4 4.9 fusion.337
  689.4 19.5 %multiply_reduce_fusion.51 = (f32[2]{0:T(128)S(1)}, f32[2,3,1024]{2,1,0:T(4,128)S(1)}) fusion(f32[2,3,1024]{2,1,0:T(4,128)} %collective-permute-done, f32[2,1024,2304]{2,1,0:T(8,128)} %constant_dynamic-update-slice_fusion.32, f32[2304,3,1]{0,1,2:T(4,128)S(1)} %copy-done.155, f32[2]{0:T(128)S(1)} %copy-done.319, f32[2,3,1024]{2,0,1:T(2,128)S(1)} %copy-done.171, ...), kind=kOutput, calls=%fused_computation.854 | convolution fusion | flops 169918464 | bytes 19000352 | tf_op jit(solution)/shard_map/jvp(vmap())/dot_general | solution.py:146
  710.2 15.2 %fusion.285 = f32[2,32,32,2304]{3,2,1,0:T(8,128)S(1)} fusion(f32[2,32,32,3]{2,1,3,0:T(8,128)S(1)} %reshape.5898, f32[2304,3,1,1]{0,1,2,3:T(4,128)S(1)} %copy-done.178), kind=kOutput, calls=%fused_computation.795 | convolution fusion | flops 169869312 | bytes 18926592 | tf_op jit(solution)/shard_map/transpose(jvp(vmap()))/dot_general | solution.py:146
  725.4 7.0 fusion.417
  732.4 3.8 pad_add_fusion.4
  737.7 4.6 pad_add_fusion.29
  752.5 4.7 multiply_reduce_fusion.1
  760.1 4.9 fusion.473
  767.7 8.1 fusion.474
  786.0 4.8 fusion.396
  795.7 6.9 fusion.416
  808.0 4.6 pad_add_fusion.23
  824.0 3.9 fusion.63
  827.9 7.1 fusion.415
  840.4 4.6 pad_add_fusion.17
  851.7 4.3 fusion.403
  859.7 6.7 fusion.414
  871.8 4.6 pad_add_fusion.11
  887.2 3.9 fusion.59
  891.2 6.7 fusion.413
  903.3 4.6 pad_add_fusion.5
  915.6 4.2 convolution_bitcast_fusion.10
  932.7 5.4 fusion.1
  938.2 5.9 fusion.3
  957.2 24.7 %add_add_fusion = f32[176,128,128]{2,1,0:T(8,128)} fusion(f32[36,128,128]{2,1,0:T(8,128)S(1)} %bitcast.1231, f32[36,128,128]{2,1,0:T(8,128)S(1)} %bitcast.1232, f32[36,128,128]{2,1,0:T(8,128)S(1)} %bitcast.1233, f32[36,128,128]{2,1,0:T(8,128)S(1)} %bitcast.1234, f32[8,128,128]{2,1,0:T(8,128)} %bitcast.1367, f32[8,128,128]{2,1,0:T(8,128)S(1)} %bitcast.1366, ...), kind=kLoop, calls=%fused_computation.5 | loop fusion | flops 43253760 | bytes 34603008 | tf_op jit(solution)/shard_map/add | solution.py:269
  981.9 18.4 %copy.552 = f32[22,8,128,128]{3,1,2,0:T(8,128)} copy(f32[22,8,128,128]{3,2,1,0:T(8,128)} %bitcast.1198) | data formatting | bytes 23068672
  1000.7 19.8 %convolution_bitcast_fusion.9 = f32[9,3,256]{2,1,0:T(4,128)S(1)} fusion(f32[9,256,2,1024]{3,1,0,2:T(8,128)} %bitcast.1196, f32[2,3,1024]{2,1,0:T(4,128)S(1)} %copy-done.167, f32[2]{0:T(128)S(1)} %copy-done.360, f32[2]{0:T(128)S(1)} %copy-done.320), kind=kOutput, calls=%fused_computation.277 | convolution fusion | flops 169887744 | bytes 18926608 | tf_op jit(solution)/shard_map/transpose(jvp(vmap()))/dot_general | solution.py:146
  1023.1 42.2 %psum.21 = f32[]{:T(128)} all-reduce(f32[]{:T(128)S(6)} %add.2360), channel_id=1, replica_groups=mesh['pair'=2,'dp'=16] {'pair','dp'}, use_global_device_ids=true, to_apply=%region_107.108 | all-reduce | flops 1 | bytes 8 | tf_op jit(solution)/shard_map/psum | solution.py:273
  1065.3 182.0 %all-reduce.191.cloned.1.call-done = (f32[176,16384]{1,0:T(8,128)}, f32[74,256]{1,0:T(8,128)}) async-done(((f32[176,16384]{1,0:T(8,128)}, f32[74,256]{1,0:T(8,128)}), (f32[176,16384]{1,0:T(8,128)}, f32[74,256]{1,0:T(8,128)})) %all-reduce.191.cloned.1.call-update) | async-done | bytes 11610128 | tf_op jit(solution)/shard_map/psum | solution.py:273
  1247.3 7.9 multiply_reduce_fusion
  1257.2 6.6 fusion.40
  (1760 shorter events, 547.5 us)
Async XLA Ops:
  7.2 1257.3 %copy-start = (f32[6,128,128]{2,1,0:T(8,128)S(1)}, f32[6,128,128]{2,1,0:T(8,128)}, u32[]{:S(2)}) copy-start(f32[6,128,128]{2,1,0:T(8,128)} %param.30) | copy-start | bytes 1179652
  7.2 91.5 %all-gather.2.cloned.1.call-start = ((), (), s32[]{:S(2)}) async-start(), calls=%async_computation | async-start | bytes 6488064 | tf_op jit(solution)/shard_map/all_gather | solution.py:223
  9.0 18.9 %copy-start.152 = (f32[74,256]{1,0:T(8,128)S(1)}, f32[74,256]{1,0:T(8,128)}, u32[]{:S(2)}) copy-start(f32[74,256]{1,0:T(8,128)} %param.31) | copy-start | bytes 227332
  9.0 1238.3 %all-reduce.191.cloned.1.call-start = ((), (), s32[]{:S(2)}) async-start(), calls=%async_computation.1 | async-start | bytes 23232512 | tf_op jit(solution)/shard_map/psum | solution.py:273
  10.6 40.4 %copy-start.188 = (f32[1,256]{1,0:T(1,128)}, f32[1,256]{1,0:T(1,128)S(1)}, u32[]{:S(2)}) copy-start(f32[1,256]{1,0:T(1,128)S(1)} %get-tuple-element.426) | copy-start | bytes 3076
  29.7 155.8 %copy-start.3 = (f32[2,1024,256]{2,1,0:T(8,128)}, f32[2,1024,256]{2,1,0:T(8,128)S(1)}, u32[]{:S(2)}) copy-start(f32[2,1024,256]{2,1,0:T(8,128)S(1)} %get-tuple-element.519) | copy-start | bytes 6291460
  51.5 38.1 %copy-start.20 = (f32[256,256]{1,0:T(8,128)}, f32[256,256]{1,0:T(8,128)S(1)}, u32[]{:S(2)}) copy-start(f32[256,256]{1,0:T(8,128)S(1)} %get-tuple-element.542) | copy-start | bytes 786436
  51.9 37.7 %copy-start.225 = (f32[256]{0:T(256)}, f32[256]{0:T(256)S(1)}, u32[]{:S(2)}) copy-start(f32[256]{0:T(256)S(1)} %sub.1010) | copy-start | bytes 3076
  52.9 36.7 %copy-start.236 = (f32[256]{0:T(256)}, f32[256]{0:T(256)S(1)}, u32[]{:S(2)}) copy-start(f32[256]{0:T(256)S(1)} %mul.3338) | copy-start | bytes 3076
  55.9 33.7 %copy-start.117 = (f32[256,256]{1,0:T(8,128)}, f32[256,256]{1,0:T(8,128)S(1)}, u32[]{:S(2)}) copy-start(f32[256,256]{1,0:T(8,128)S(1)} %get-tuple-element.544) | copy-start | bytes 786436
  98.7 17.7 %copy-start.323 = (bf16[2,128]{1,0:T(2,128)(2,1)}, bf16[2,128]{1,0:T(2,128)(2,1)S(1)}, u32[]{:S(2)}) copy-start(bf16[2,128]{1,0:T(2,128)(2,1)S(1)} %get-tuple-element.500) | copy-start | bytes 1540
  98.7 17.6 %copy-start.325 = (bf16[2,128]{1,0:T(2,128)(2,1)}, bf16[2,128]{1,0:T(2,128)(2,1)S(1)}, u32[]{:S(2)}) copy-start(bf16[2,128]{1,0:T(2,128)(2,1)S(1)} %get-tuple-element.501) | copy-start | bytes 1540
  120.9 18.1 %copy-start.280 = (f32[1,256]{1,0:T(1,128)S(1)}, f32[1,256]{1,0:T(1,128)}, u32[]{:S(2)}) copy-start(f32[1,256]{1,0:T(1,128)} %get-tuple-element.423) | copy-start | bytes 3076
  269.2 258.9 %copy-start.1 = (f32[2,1024,256]{2,1,0:T(8,128)}, f32[2,1024,256]{2,1,0:T(8,128)S(1)}, u32[]{:S(2)}) copy-start(f32[2,1024,256]{2,1,0:T(8,128)S(1)} %get-tuple-element.532) | copy-start | bytes 6291460
  270.7 31.9 %copy-start.201 = (f32[2,256]{1,0:T(2,128)}, f32[2,256]{1,0:T(2,128)S(1)}, u32[]{:S(2)}) copy-start(f32[2,256]{1,0:T(2,128)S(1)} %mul.3232) | copy-start | bytes 6148
  271.1 108.3 %copy-start.30 = (bf16[2,6,128,128]{2,0,3,1:T(2,128)(2,1)}, bf16[2,6,128,128]{2,0,3,1:T(2,128)(2,1)S(1)}, u32[]{:S(2)}) copy-start(bf16[2,6,128,128]{2,0,3,1:T(2,128)(2,1)S(1)} %copy.186) | copy-start | bytes 1179652
  319.5 18.0 %copy-start.156 = (bf16[1,16,16,256]{3,2,1,0:T(8,128)(2,1)S(1)}, bf16[1,16,16,256]{3,2,1,0:T(8,128)(2,1)}, u32[]{:S(2)}) copy-start(bf16[1,16,16,256]{3,2,1,0:T(8,128)(2,1)} %get-tuple-element.369) | copy-start | bytes 393220
  408.2 20.7 %copy-start.132 = (bf16[256,256,1]{1,0,2:T(8,128)(2,1)}, bf16[256,256,1]{1,0,2:T(8,128)(2,1)S(1)}, u32[]{:S(2)}) copy-start(bf16[256,256,1]{1,0,2:T(8,128)(2,1)S(1)} %reshape.5847) | copy-start | bytes 393220
  472.7 216.6 %collective-permute-start = (f32[2,3,1024]{2,1,0:T(4,128)}, f32[2,3,1024]{2,1,0:T(4,128)}, u32[]{:S(2)}, u32[]{:S(2)}) collective-permute-start(f32[2,3,1024]{2,1,0:T(4,128)} %fusion.120), channel_id=1, source_target_pairs={{0,16},{16,0},{1,17},{17,1},{2,18},{18,2},{3,19},{19,3},{4,20},{20... | collective-permute-start | bytes 73736 | tf_op jit(solution)/shard_map/ppermute | solution.py:34
  516.5 89.9 %collective-permute-start.1 = (f32[1,3,256]{2,1,0:T(4,128)S(1)}, f32[1,3,256]{2,1,0:T(4,128)S(1)}, u32[]{:S(2)}, u32[]{:S(2)}) collective-permute-start(f32[1,3,256]{2,1,0:T(4,128)S(1)} %fusion.139), channel_id=1, source_target_pairs={{0,16},{16,0},{1,17},{17,1},{2,18},{18,2},{3,19},{19,3},{4,20},{20... | collective-permute-start | bytes 9224 | tf_op jit(solution)/shard_map/ppermute | solution.py:34
  587.3 19.1 %copy-start.253 = (f32[1,3,256]{2,0,1:T(1,128)S(1)}, f32[1,3,256]{2,0,1:T(1,128)}, u32[]{:S(2)}) copy-start(f32[1,3,256]{2,0,1:T(1,128)} %copy-done.252) | copy-start | bytes 9220
  587.3 19.1 %copy-start.255 = (f32[1,3,256]{2,0,1:T(1,128)S(1)}, f32[1,3,256]{2,0,1:T(1,128)}, u32[]{:S(2)}) copy-start(f32[1,3,256]{2,0,1:T(1,128)} %copy-done.254) | copy-start | bytes 9220
  587.3 19.1 %copy-start.298 = (f32[1,256]{1,0:T(1,128)S(1)}, f32[1,256]{1,0:T(1,128)}, u32[]{:S(2)}) copy-start(f32[1,256]{1,0:T(1,128)} %fusion.358) | copy-start | bytes 3076
  689.4 19.5 %copy-start.403 = (f32[4]{0:T(128)S(1)}, f32[4]{0:T(128)}, u32[]{:S(2)}) copy-start(f32[4]{0:T(128)} %copy-done.402) | copy-start | bytes 52
  689.4 20.8 %copy-start.178 = (f32[2304,3,1,1]{0,1,2,3:T(4,128)S(1)}, f32[2304,3,1,1]{0,1,2,3:T(4,128)}, u32[]{:S(2)}) copy-start(f32[2304,3,1,1]{0,1,2,3:T(4,128)} %reshape.5859) | copy-start | bytes 82948
  981.9 18.4 %copy-start.167 = (f32[2,3,1024]{2,1,0:T(4,128)S(1)}, f32[2,3,1024]{2,1,0:T(4,128)}, u32[]{:S(2)}) copy-start(f32[2,3,1024]{2,1,0:T(4,128)} %copy-done.166) | copy-start | bytes 73732
  981.9 18.4 %copy-start.320 = (f32[2]{0:T(128)S(1)}, f32[2]{0:T(128)}, u32[]{:S(2)}) copy-start(f32[2]{0:T(128)} %get-tuple-element.508) | copy-start | bytes 28
  981.9 18.4 %copy-start.360 = (f32[2]{0:T(128)S(1)}, f32[2]{0:T(128)}, u32[]{:S(2)}) copy-start(f32[2]{0:T(128)} %copy-done.359) | copy-start | bytes 28
  1000.3 20.2 %copy-start.179 = (f32[27,256]{1,0:T(8,128)S(1)}, f32[27,256]{1,0:T(8,128)}, u32[]{:S(2)}) copy-start(f32[27,256]{1,0:T(8,128)} %convolution_bitcast_fusion.10) | copy-start | bytes 82948
  1000.3 20.2 %copy-start.180 = (f32[27,256]{1,0:T(8,128)S(1)}, f32[27,256]{1,0:T(8,128)}, u32[]{:S(2)}) copy-start(f32[27,256]{1,0:T(8,128)} %fusion.301) | copy-start | bytes 82948
  1000.3 20.2 %copy-start.181 = (f32[27,256]{1,0:T(8,128)S(1)}, f32[27,256]{1,0:T(8,128)}, u32[]{:S(2)}) copy-start(f32[27,256]{1,0:T(8,128)} %reshape.5826) | copy-start | bytes 82948
  1000.4 20.2 %copy-start.339 = (f32[256]{0:T(256)S(1)}, f32[256]{0:T(256)}, u32[]{:S(2)}) copy-start(f32[256]{0:T(256)} %get-tuple-element.89) | copy-start | bytes 3076
  1000.4 20.2 %copy-start.340 = (f32[256]{0:T(256)S(1)}, f32[256]{0:T(256)}, u32[]{:S(2)}) copy-start(f32[256]{0:T(256)} %get-tuple-element.35) | copy-start | bytes 3076
  1000.4 20.2 %copy-start.341 = (f32[256]{0:T(256)S(1)}, f32[256]{0:T(256)}, u32[]{:S(2)}) copy-start(f32[256]{0:T(256)} %get-tuple-element.93) | copy-start | bytes 3076
  1000.4 20.2 %copy-start.342 = (f32[256]{0:T(256)S(1)}, f32[256]{0:T(256)}, u32[]{:S(2)}) copy-start(f32[256]{0:T(256)} %get-tuple-element.37) | copy-start | bytes 3076
  1000.4 20.2 %copy-start.363 = (f32[256]{0:T(256)S(1)}, f32[256]{0:T(256)}, u32[]{:S(2)}) copy-start(f32[256]{0:T(256)} %get-tuple-element.206) | copy-start | bytes 3076
  1000.4 20.2 %copy-start.364 = (f32[256]{0:T(256)S(1)}, f32[256]{0:T(256)}, u32[]{:S(2)}) copy-start(f32[256]{0:T(256)} %get-tuple-element.67) | copy-start | bytes 3076
  1000.4 20.2 %copy-start.365 = (f32[256]{0:T(256)S(1)}, f32[256]{0:T(256)}, u32[]{:S(2)}) copy-start(f32[256]{0:T(256)} %get-tuple-element.39) | copy-start | bytes 3076
  1000.4 20.2 %copy-start.366 = (f32[256]{0:T(256)S(1)}, f32[256]{0:T(256)}, u32[]{:S(2)}) copy-start(f32[256]{0:T(256)} %get-tuple-element.579) | copy-start | bytes 3076
  1000.4 20.2 %copy-start.367 = (f32[256]{0:T(256)S(1)}, f32[256]{0:T(256)}, u32[]{:S(2)}) copy-start(f32[256]{0:T(256)} %get-tuple-element.45) | copy-start | bytes 3076
  1000.5 20.2 %copy-start.368 = (f32[256]{0:T(256)S(1)}, f32[256]{0:T(256)}, u32[]{:S(2)}) copy-start(f32[256]{0:T(256)} %get-tuple-element.301) | copy-start | bytes 3076
  1000.5 20.2 %copy-start.369 = (f32[256]{0:T(256)S(1)}, f32[256]{0:T(256)}, u32[]{:S(2)}) copy-start(f32[256]{0:T(256)} %get-tuple-element.71) | copy-start | bytes 3076
  1000.5 20.2 %copy-start.370 = (f32[256]{0:T(256)S(1)}, f32[256]{0:T(256)}, u32[]{:S(2)}) copy-start(f32[256]{0:T(256)} %get-tuple-element.41) | copy-start | bytes 3076
  1000.5 20.2 %copy-start.371 = (f32[256]{0:T(256)S(1)}, f32[256]{0:T(256)}, u32[]{:S(2)}) copy-start(f32[256]{0:T(256)} %get-tuple-element.303) | copy-start | bytes 3076
  1000.5 20.2 %copy-start.372 = (f32[256]{0:T(256)S(1)}, f32[256]{0:T(256)}, u32[]{:S(2)}) copy-start(f32[256]{0:T(256)} %get-tuple-element.73) | copy-start | bytes 3076
  1000.5 20.2 %copy-start.373 = (f32[256]{0:T(256)S(1)}, f32[256]{0:T(256)}, u32[]{:S(2)}) copy-start(f32[256]{0:T(256)} %get-tuple-element.43) | copy-start | bytes 3076
  1000.5 20.2 %copy-start.374 = (f32[256]{0:T(256)S(1)}, f32[256]{0:T(256)}, u32[]{:S(2)}) copy-start(f32[256]{0:T(256)} %get-tuple-element.49) | copy-start | bytes 3076
  1000.5 20.2 %copy-start.375 = (f32[256]{0:T(256)S(1)}, f32[256]{0:T(256)}, u32[]{:S(2)}) copy-start(f32[256]{0:T(256)} %get-tuple-element.50) | copy-start | bytes 3076
  1000.5 20.2 %copy-start.378 = (f32[256]{0:T(256)S(1)}, f32[256]{0:T(256)}, u32[]{:S(2)}) copy-start(f32[256]{0:T(256)} %get-tuple-element.21) | copy-start | bytes 3076
  1000.5 20.2 %copy-start.379 = (f32[256]{0:T(256)S(1)}, f32[256]{0:T(256)}, u32[]{:S(2)}) copy-start(f32[256]{0:T(256)} %get-tuple-element.23) | copy-start | bytes 3076
  1000.5 20.2 %copy-start.380 = (f32[256]{0:T(256)S(1)}, f32[256]{0:T(256)}, u32[]{:S(2)}) copy-start(f32[256]{0:T(256)} %get-tuple-element.583) | copy-start | bytes 3076
  1000.6 20.2 %copy-start.381 = (f32[256]{0:T(256)S(1)}, f32[256]{0:T(256)}, u32[]{:S(2)}) copy-start(f32[256]{0:T(256)} %get-tuple-element.9) | copy-start | bytes 3076
  1000.6 20.2 %copy-start.382 = (f32[256]{0:T(256)S(1)}, f32[256]{0:T(256)}, u32[]{:S(2)}) copy-start(f32[256]{0:T(256)} %get-tuple-element.26) | copy-start | bytes 3076
  1000.6 20.2 %copy-start.383 = (f32[256]{0:T(256)S(1)}, f32[256]{0:T(256)}, u32[]{:S(2)}) copy-start(f32[256]{0:T(256)} %get-tuple-element.11) | copy-start | bytes 3076
  1000.6 20.2 %copy-start.384 = (f32[256]{0:T(256)S(1)}, f32[256]{0:T(256)}, u32[]{:S(2)}) copy-start(f32[256]{0:T(256)} %get-tuple-element.32) | copy-start | bytes 3076
  1000.6 20.2 %copy-start.385 = (f32[256]{0:T(256)S(1)}, f32[256]{0:T(256)}, u32[]{:S(2)}) copy-start(f32[256]{0:T(256)} %get-tuple-element.19) | copy-start | bytes 3076
  1000.6 20.2 %copy-start.386 = (f32[256]{0:T(256)S(1)}, f32[256]{0:T(256)}, u32[]{:S(2)}) copy-start(f32[256]{0:T(256)} %get-tuple-element.34) | copy-start | bytes 3076
  1000.6 20.2 %copy-start.387 = (f32[256]{0:T(256)S(1)}, f32[256]{0:T(256)}, u32[]{:S(2)}) copy-start(f32[256]{0:T(256)} %get-tuple-element.30) | copy-start | bytes 3076
  1000.6 20.2 %copy-start.388 = (f32[256]{0:T(256)S(1)}, f32[256]{0:T(256)}, u32[]{:S(2)}) copy-start(f32[256]{0:T(256)} %get-tuple-element.31) | copy-start | bytes 3076
  1000.6 20.2 %copy-start.395 = (f32[256]{0:T(256)S(1)}, f32[256]{0:T(256)}, u32[]{:S(2)}) copy-start(f32[256]{0:T(256)} %get-tuple-element.69) | copy-start | bytes 3076
  1000.6 20.2 %copy-start.396 = (f32[256]{0:T(256)S(1)}, f32[256]{0:T(256)}, u32[]{:S(2)}) copy-start(f32[256]{0:T(256)} %get-tuple-element.300) | copy-start | bytes 3076
  1000.7 20.2 %copy-start.397 = (f32[256]{0:T(256)S(1)}, f32[256]{0:T(256)}, u32[]{:S(2)}) copy-start(f32[256]{0:T(256)} %get-tuple-element.13) | copy-start | bytes 3076
  1000.7 20.2 %copy-start.398 = (f32[256]{0:T(256)S(1)}, f32[256]{0:T(256)}, u32[]{:S(2)}) copy-start(f32[256]{0:T(256)} %get-tuple-element.28) | copy-start | bytes 3076
  1000.7 20.2 %copy-start.399 = (f32[256]{0:T(256)S(1)}, f32[256]{0:T(256)}, u32[]{:S(2)}) copy-start(f32[256]{0:T(256)} %get-tuple-element.15) | copy-start | bytes 3076
  (372 other events, 1356.3 us)
Sparse Core Ops, SparseCore 0:
  11.5 72.3 all-gather.1
  1022.5 224.7 all-reduce.190
where the time goes:
time: 1290 us; the launch traced here: 1280 us
  local copies, waits for them, and re-layouts  471 us (37%)
  matrix products  295 us (23%)
  other arithmetic  239 us (19%)
  waiting for transfers between devices  182 us (14%)
  blocking collectives  42.2 us (3%)
  between operations  32.5 us (3%)
    psum x1, waiting for transfers between devices, local(): lax.psum((flat, vec_grad, loss_part), ('pair', 'dp'))  182 us
    unnamed x1012, local copies, waits for them, and re-layouts  147 us
    dot_general x37, matrix products, product_plain(): jnp.dot(left.astype(jnp.bfloat16), right.astype(jnp.bfloat16), preferred_...  97.8 us
    dot_general x8, matrix products, network(): return jnp.dot(patches(active, side), head, precision=HIGH)  84.6 us
    dot_general x34, matrix products, product_low(): return rounded_product(left, right)  82 us
    dot_general x17, local copies, waits for them, and re-layouts, product_low(): return rounded_product(left, right)  64.6 us
    convert_element_type x17, local copies, waits for them, and re-layouts, product_plain(): right.astype(jnp.bfloat16)  46.9 us
    add_any x15, other arithmetic, patches(): padded[offset_y:offset_y + side, offset_x:offset_x + side]  42.4 us
  transfers between devices with their start and end apart: 4, of which 1 were waited for; matrix products, arithmetic and copies ran while one was open for 22% of the time, Pallas kernels for 0%

commit v1 on v0

v1 whole, which is shorter than its diff:
```python
from functools import partial
import math

import jax
import jax.numpy as jnp
from jax import lax
from jax.experimental import pallas as pl
from jax.experimental.pallas import tpu as pltpu
from jax.sharding import PartitionSpec as P

GROUPS = 32
SIDE = 32
SMALL_SIDE = 16
NSTEPS = 11
STEP = 10
CH = 256
BLOCK = 128

HIGH = lax.Precision.HIGHEST
SIGMA_DATA = 0.5
SIGMA_MIN = 0.002
SIGMA_MAX = 80.0
RHO = 7.0
HUBER = 0.00054
CLIP = 1.0
BETA_ONE = 0.9
BETA_TWO = 0.999
DECAY = 0.0001
RATE_MATRIX = 0.02
RATE_VECTOR = 0.02
ROOT_HALF = 1.0 / math.sqrt(2.0)
ANY = pl.ANY
F32 = jnp.float32
BF16 = jnp.bfloat16

CONV_BLOCKS = 36
TIME_FIRST, TIME_COUNT = 144, 8
TRIPLE_FIRST, TRIPLE_COUNT = 160, 12
PROJ_FIRST, PROJ_COUNT = 172, 4

ROWS = 128
MM_ROWS = 256


def mm(left, right):
    return jnp.dot(left, right, preferred_element_type=F32)


def mm_nt(left, right):
    return lax.dot_general(left, right, (((1,), (1,)), ((), ())), preferred_element_type=F32)


def mm_tn(left, right):
    return lax.dot_general(left, right, (((0,), (0,)), ((), ())), preferred_element_type=F32)


def split(value):
    high = value.astype(BF16)
    return high, (value - high.astype(F32)).astype(BF16)


def fold(value):
    return jnp.sum(value.reshape(value.shape[0] // 8, 8, value.shape[1]), axis=0)


def over_rows(value):
    return jnp.sum(value, axis=0, keepdims=True)


def group_sum(value):
    value = jnp.broadcast_to(value, (8, CH))
    lane = lax.broadcasted_iota(jnp.int32, (8, CH), 1)
    for step in (1, 2, 4):
        other = jnp.where(
            (lane & step) != 0, pltpu.roll(value, step, 1), pltpu.roll(value, CH - step, 1)
        )
        value = value + other
    return value[0:1]


def sigmoid(value):
    return 1.0 / (1.0 + jnp.exp(-value))


def group_stats(ref, pixels):
    scale = 1.0 / (8 * pixels)
    total = jnp.zeros((8, CH), F32)
    for row in range(0, pixels, ROWS):
        total = total + fold(ref[row : row + ROWS, :])
    mean = group_sum(over_rows(total)) * scale
    total = jnp.zeros((8, CH), F32)
    for row in range(0, pixels, ROWS):
        center = ref[row : row + ROWS, :] - mean
        total = total + fold(center * center)
    return mean, lax.rsqrt(group_sum(over_rows(total)) * scale + 1e-06)


def write_shifted(ref, row, value, side):
    count = value.shape[0]
    column = lax.broadcasted_iota(jnp.int32, (count, CH), 0) & (side - 1)
    left = jnp.where(column == 0, 0.0, pltpu.roll(value, 1, 0))
    right = jnp.where(column == side - 1, 0.0, pltpu.roll(value, count - 1, 0))
    at = slice(side + row, side + row + count)
    ref[at, 0:CH] = left.astype(BF16)
    ref[at, CH : 2 * CH] = value.astype(BF16)
    ref[at, 2 * CH : 3 * CH] = right.astype(BF16)


def clear_ends(ref, side):
    pixels = side * side
    zeros = jnp.zeros((side, 3 * CH), BF16)
    ref[0:side, :] = zeros
    ref[side + pixels : 2 * side + pixels, :] = zeros


def tap_shifts(side):
    pixels = side * side
    place = lax.broadcasted_iota(jnp.int32, (8, pixels), 1)
    x = place & (side - 1)
    y = place >> (side.bit_length() - 1)
    taps = []
    for dy in (-1, 0, 1):
        for dx in (-1, 0, 1):
            inside = (x + dx >= 0) & (x + dx < side) & (y + dy >= 0) & (y + dy < side)
            taps.append((dy * side + dx, inside))
    return taps


def net_kernel(
    owner_ref,
    scal_ref,
    emb_ref,
    big_ref,
    big_noise_ref,
    small_ref,
    small_noise_ref,
    mask_ref,
    vec_ref,
    vin_ref,
    head_ref,
    whole_ref,
    grads_ref,
    gvec_ref,
    gin_ref,
    ghead_ref,
    loss_ref,
    conv_w,
    time_w,
    triple_w,
    proj_w,
    conv_g,
    time_g,
    triple_g,
    proj_g,
    stage,
    hid_t,
    hid_s,
    first_t,
    first_s,
    pat_t,
    pat_s,
    gpat,
    grad_t,
    probs,
    keep,
    keep_t,
    normed,
    mixed,
    act_hi,
    act_lo,
    dhid,
    dact,
    dtri,
    tsh,
    gtime,
    x80,
    sem,
):
    bigs = big_ref.shape[0]
    smalls = small_ref.shape[0]
    count = bigs + smalls

    def block_copy(index, target):
        return pltpu.make_async_copy(whole_ref.at[owner_ref[index]], target, sem)

    def conv_target(array, index):
        m = index // CONV_BLOCKS
        rest = index - m * CONV_BLOCKS
        i = rest // 2
        j = rest - i * 2
        return array.at[m, pl.ds(pl.multiple_of(i * BLOCK, BLOCK), BLOCK), pl.ds(pl.multiple_of(j * BLOCK, BLOCK), BLOCK)]

    def load_conv(index, _):
        block_copy(index, conv_target(conv_w, index)).start()
        return _

    lax.fori_loop(0, 4 * CONV_BLOCKS, load_conv, 0)
    others = []
    for number in range(2):
        for k in range(TIME_COUNT):
            i, j = k // 4, k % 4
            others.append((TIME_FIRST + TIME_COUNT * number + k, time_w.at[number, i * BLOCK : (i + 1) * BLOCK, j * BLOCK : (j + 1) * BLOCK]))
    for k in range(TRIPLE_COUNT):
        i, j = k // 6, k % 6
        others.append((TRIPLE_FIRST + k, triple_w.at[i * BLOCK : (i + 1) * BLOCK, j * BLOCK : (j + 1) * BLOCK]))
    for k in range(PROJ_COUNT):
        i, j = k // 2, k % 2
        others.append((PROJ_FIRST + k, proj_w.at[i * BLOCK : (i + 1) * BLOCK, j * BLOCK : (j + 1) * BLOCK]))
    for index, target in others:
        block_copy(index, target).start()

    conv_g[...] = jnp.zeros_like(conv_g)
    triple_g[...] = jnp.zeros_like(triple_g)
    proj_g[...] = jnp.zeros_like(proj_g)
    gvec_ref[...] = jnp.zeros_like(gvec_ref)
    gin_ref[...] = jnp.zeros_like(gin_ref)
    ghead_ref[...] = jnp.zeros_like(ghead_ref)
    loss_ref[...] = jnp.zeros_like(loss_ref)
    gtime[...] = jnp.zeros_like(gtime)

    vin_hi, vin_lo = split(vin_ref[...])
    vin3 = jnp.concatenate([vin_hi, vin_lo, vin_hi], axis=0)
    head_hi, head_lo = split(head_ref[...])
    head2 = jnp.concatenate([head_hi, head_lo], axis=0)
    head3 = jnp.concatenate([head_hi, head_lo, head_hi], axis=0)

    def wait_conv(index, _):
        block_copy(0, conv_target(conv_w, index)).wait()
        return _

    lax.fori_loop(0, 4 * CONV_BLOCKS, wait_conv, 0)
    for index, target in others:
        block_copy(index, target).wait()

    for number in range(2):
        tsh[number] = mm(emb_ref[...], time_w[number])

    def vec(row):
        return vec_ref[row : row + 1, :]

    def add_vec(row, value):
        gvec_ref[row : row + 1, :] += value

    def run(image, clean_ref, noise_ref, local, side, small):
        pixels = side * side
        taps = tap_shifts(side)

        def scal(which, item):
            return scal_ref[image * 16 + which * 4 + item]

        def chunks(step=ROWS):
            return range(0, pixels, min(step, pixels))

        rows = min(ROWS, pixels)
        mrows = min(MM_ROWS, pixels)

        clear_ends(pat_t, side)
        for k in range(4):
            clear_ends(pat_s.at[k], side)
        clear_ends(gpat, side)

        noisies = []
        for which in range(2):
            noisies.append(clean_ref[local] + scal(which, 0) * noise_ref[local])

        def shifted_input(which):
            scaled = noisies[which] * scal(which, 1)
            parts = []
            for shift, inside in taps:
                parts.append(jnp.where(inside, pltpu.roll(scaled, (-shift) % pixels, 1), 0.0))
            first = lax.broadcasted_iota(jnp.int32, (8, pixels), 0) == 0
            parts.append(jnp.where(first, 1.0, 0.0))
            return jnp.concatenate(parts, axis=0)

        def hid(which, level):
            return hid_t if which == 0 else hid_s.at[level]

        def pat(which, level):
            return pat_t if which == 0 else pat_s.at[level]

        def first(which, level):
            return first_t if which == 0 else first_s.at[level]

        for which in range(2):
            value = shifted_input(which)
            high, low = split(value)
            if which == 1:
                x80[0:80, 0:pixels] = high
                x80[80:160, 0:pixels] = low
            three = jnp.concatenate([high, high, low], axis=0)
            hid(which, 0)[0:pixels, :] = mm_tn(three, vin3)

        def shifts(which, number):
            row = tsh[number, pl.ds(2 * image + which, 1), :]
            return row[:, 0:CH], row[:, CH:]

        stats = {}

        def act(which, key, src, gain, bias, dst):
            mean, rstd = group_stats(src, pixels)
            if which == 1:
                stats[key] = (mean, rstd)
            scale = rstd * gain
            for row in chunks():
                z = (src[row : row + rows, :] - mean) * scale + bias
                write_shifted(dst, row, z * sigmoid(z), side)

        def conv(src, number, row):
            total = None
            for dy in range(3):
                part = mm(src[dy * side + row : dy * side + row + mrows, :], conv_w[number, dy * 768 : (dy + 1) * 768, :])
                total = part if total is None else total + part
            return total

        for number in range(2):
            base = 28 + 6 * number
            for which in range(2):
                act(which, ("a", number), hid(which, number), vec(base), vec(base + 1), pat(which, 2 * number))
            for which in range(2):
                for row in chunks(MM_ROWS):
                    first(which, number)[row : row + mrows, :] = conv(pat(which, 2 * number), 2 * number, row) + vec(base + 2)
            for which in range(2):
                gain_t, bias_t = shifts(which, number)
                act(
                    which,
                    ("b", number),
                    first(which, number),
                    1.0 + gain_t + vec(base + 3),
                    bias_t + vec(base + 4),
                    pat(which, 2 * number + 1),
                )
            for which in range(2):
                for row in chunks(MM_ROWS):
                    second = conv(pat(which, 2 * number + 1), 2 * number + 1, row) + vec(base + 5)
                    at = slice(row, row + mrows)
                    hid(which, number + 1)[at, :] = (hid(which, number)[at, :] + second) * ROOT_HALF

        results = []
        for which in range(2):
            src = hid(which, 2)
            mean, rstd = group_stats(src, pixels)
            if which == 1:
                stats["n"] = (mean, rstd)
            scale = rstd * vec(40)
            for row in chunks():
                value = (src[row : row + rows, :] - mean) * scale + vec(41)
                normed[row : row + rows, :] = value.astype(BF16)
            for row in chunks(MM_ROWS):
                at = slice(row, row + mrows)
                triple = mm(normed[at, :], triple_w[...])
                keep[0, at, :] = (triple[:, 0:CH] + vec(42)).astype(BF16)
                key = triple[:, CH : 2 * CH]
                value = triple[:, 2 * CH :] + vec(43)
                keep[1, at, :] = key.astype(BF16)
                keep[2, at, :] = value.astype(BF16)
                keep_t[0, :, at] = jnp.transpose(value).astype(BF16)
                if which == 1:
                    keep_t[1, :, at] = jnp.transpose(key).astype(BF16)
            for col in chunks(MM_ROWS):
                at = slice(col, col + mrows)
                scores = mm_nt(keep[1, 0:pixels, :], keep[0, at, :]) * (1.0 / math.sqrt(CH))
                top = jnp.max(scores, axis=0, keepdims=True)
                weight = jnp.exp(scores - top)
                weight = weight * (1.0 / jnp.sum(weight, axis=0, keepdims=True))
                if which == 1:
                    probs[0:pixels, at] = weight
                out_t = mm(keep_t[0, :, 0:pixels], weight.astype(BF16))
                mixed[at, :] = jnp.transpose(out_t).astype(BF16)
            for row in chunks(MM_ROWS):
                at = slice(row, row + mrows)
                value = mm(mixed[at, :], proj_w[...]) + vec(44)
                hid(which, 3)[at, :] = (hid(which, 2)[at, :] + value) * ROOT_HALF
            src = hid(which, 3)
            mean, rstd = group_stats(src, pixels)
            if which == 1:
                stats["h"] = (mean, rstd)
            scale = rstd * vec(45)
            for row in chunks():
                z = (src[row : row + rows, :] - mean) * scale + vec(46)
                high, low = split(z * sigmoid(z))
                act_hi[row : row + rows, :] = high
                act_lo[row : row + rows, :] = low
            wide = mm_nt(head2, act_hi[0:pixels, :])
            wide = wide[0:80] + wide[80:160] + mm_nt(head_hi, act_lo[0:pixels, :])
            out = jnp.zeros((8, pixels), F32)
            for k, (shift, inside) in enumerate(taps):
                out = out + jnp.where(inside, pltpu.roll(wide[8 * k : 8 * k + 8], (-shift) % pixels, 1), 0.0)
            results.append(scal(which, 2) * noisies[which] + scal(which, 3) * out)

        diff = results[1] - results[0]
        weighted = diff * mask_ref[local] if small else diff
        bound = HUBER * math.sqrt(3 * pixels)
        total = jnp.sum(jnp.sum(weighted * diff, axis=1, keepdims=True), axis=0, keepdims=True)
        root = jnp.sqrt(total + bound * bound)
        rate = scal(2, 0)
        loss_ref[...] += jnp.broadcast_to((root - bound) * rate, (8, 128))
        dout = weighted * ((rate * scal(1, 3)) / root)

        parts = []
        for shift, inside in taps:
            parts.append(pltpu.roll(jnp.where(inside, dout, 0.0), shift % pixels, 1))
        parts.append(jnp.zeros((8, pixels), F32))
        high, low = split(jnp.concatenate(parts, axis=0))
        two = jnp.concatenate([high, low], axis=0)
        three = jnp.concatenate([high, high, low], axis=0)
        wide = mm(two, act_hi[0:pixels, :])
        ghead_ref[...] += wide[0:80] + wide[80:160] + mm(high, act_lo[0:pixels, :])
        dact[0:pixels, :] = mm_tn(three, head3)

        scale8 = 1.0 / (8 * pixels)

        def act_back(key, src, gain, bias, active):
            mean, rstd = stats[key]
            sum_b = jnp.zeros((8, CH), F32)
            sum_g = jnp.zeros((8, CH), F32)
            for row in chunks():
                at = slice(row, row + rows)
                value = (src[at, :] - mean) * rstd
                grad = dact[at, :]
                if active:
                    z = value * gain + bias
                    sig = sigmoid(z)
                    grad = grad * (sig * (1.0 + z * (1.0 - sig)))
                    dact[at, :] = grad
                sum_b = sum_b + fold(grad)
                sum_g = sum_g + fold(grad * value)
            sum_b = over_rows(sum_b)
            sum_g = over_rows(sum_g)
            mean_b = group_sum(sum_b * gain) * scale8
            mean_g = group_sum(sum_g * gain) * scale8

            def final(row):
                at = slice(row, row + rows)
                value = (src[at, :] - mean) * rstd
                return rstd * (gain * dact[at, :] - mean_b - value * mean_g)

            return sum_b, sum_g, final

        sum_b, sum_g, final = act_back("h", hid_s.at[3], vec(45), vec(46), True)
        add_vec(45, sum_g)
        add_vec(46, sum_b)
        total = jnp.zeros((8, CH), F32)
        for row in chunks():
            at = slice(row, row + rows)
            grad = final(row) * ROOT_HALF
            dhid[at, :] = grad
            total = total + fold(grad)
            low = grad.astype(BF16)
            normed_g = low
            gpat[row : row + rows, 0:CH] = normed_g
            grad_t[0, :, at] = jnp.transpose(grad).astype(BF16)
        add_vec(44, over_rows(total))
        proj_g[...] += mm(grad_t[0, :, 0:pixels], mixed[0:pixels, :])
        for row in chunks(MM_ROWS):
            at = slice(row, row + mrows)
            gpat[at, CH : 2 * CH] = mm_nt(gpat[at, 0:CH], proj_w[...]).astype(BF16)
        total = jnp.zeros((8, CH), F32)
        for col in chunks(MM_ROWS):
            at = slice(col, col + mrows)
            grad = mm_nt(keep[2, 0:pixels, :], gpat[at, CH : 2 * CH])
            weight = probs[0:pixels, at]
            inner = jnp.sum(weight * grad, axis=0, keepdims=True)
            probs_g = (weight * (grad - inner) * (1.0 / math.sqrt(CH))).astype(BF16)
            stage[0:pixels, at] = probs_g
            stage[0:pixels, 1024 + col : 1024 + col + mrows] = weight.astype(BF16)
            dq_t = mm(keep_t[1, :, 0:pixels], probs_g)
            dtri[at, 0:CH] = jnp.transpose(dq_t).astype(BF16)
            grad_t[0, :, at] = dq_t.astype(BF16)
            total = total + fold(jnp.transpose(dq_t))
        add_vec(42, over_rows(total))
        total = jnp.zeros((8, CH), F32)
        for row in chunks(MM_ROWS):
            at = slice(row, row + mrows)
            dk = mm(stage[at, 0:pixels], keep[0, 0:pixels, :])
            dv = mm(stage[at, 1024 : 1024 + pixels], gpat[0:pixels, CH : 2 * CH])
            total = total + fold(dv)
            dtri[at, CH : 2 * CH] = dk.astype(BF16)
            dtri[at, 2 * CH :] = dv.astype(BF16)
            grad_t[1, :, at] = jnp.transpose(dk).astype(BF16)
            grad_t[2, :, at] = jnp.transpose(dv).astype(BF16)
        add_vec(43, over_rows(total))
        for part in range(3):
            triple_g[part * CH : (part + 1) * CH, :] += mm(grad_t[part, :, 0:pixels], normed[0:pixels, :])
        for row in chunks(MM_ROWS):
            at = slice(row, row + mrows)
            dact[at, :] = mm_nt(dtri[at, :], triple_w[...])
        clear_ends(gpat, side)
        sum_b, sum_g, final = act_back("n", hid_s.at[2], vec(40), vec(41), False)
        add_vec(40, sum_g)
        add_vec(41, sum_b)
        for row in chunks():
            at = slice(row, row + rows)
            dhid[at, :] += final(row)

        def conv_back(number):
            for dy in range(3):
                conv_g[number, :, dy * 768 : (dy + 1) * 768] += mm(
                    grad_t[0, :, 0:pixels], pat_s[number, dy * side : dy * side + pixels, :]
                )
            for row in chunks(MM_ROWS):
                total = None
                for dy in range(3):
                    for dx in range(3):
                        tap = dy * 3 + dx
                        start = (2 - dy) * side + row
                        part = mm_nt(
                            gpat[start : start + mrows, (2 - dx) * CH : (3 - dx) * CH],
                            conv_w[number, tap * CH : (tap + 1) * CH, :],
                        )
                        total = part if total is None else total + part
                dact[row : row + mrows, :] = total

        for number in (1, 0):
            base = 28 + 6 * number
            total = jnp.zeros((8, CH), F32)
            for row in chunks():
                at = slice(row, row + rows)
                grad = dhid[at, :] * ROOT_HALF
                dhid[at, :] = grad
                total = total + fold(grad)
                write_shifted(gpat, row, grad, side)
                grad_t[0, :, at] = jnp.transpose(grad).astype(BF16)
            add_vec(base + 5, over_rows(total))
            conv_back(2 * number + 1)
            gain_t, bias_t = shifts(1, number)
            sum_b, sum_g, final = act_back(
                ("b", number),
                first_s.at[number],
                1.0 + gain_t + vec(base + 3),
                bias_t + vec(base + 4),
                True,
            )
            add_vec(base + 3, sum_g)
            add_vec(base + 4, sum_b)
            gtime[number, pl.ds(image, 1), 0:CH] = sum_g
            gtime[number, pl.ds(image, 1), CH:] = sum_b
            total = jnp.zeros((8, CH), F32)
            for row in chunks():
                at = slice(row, row + rows)
                grad = final(row)
                total = total + fold(grad)
                write_shifted(gpat, row, grad, side)
                grad_t[0, :, at] = jnp.transpose(grad).astype(BF16)
            add_vec(base + 2, over_rows(total))
            conv_back(2 * number)
            sum_b, sum_g, final = act_back(("a", number), hid_s.at[number], vec(base), vec(base + 1), True)
            add_vec(base, sum_g)
            add_vec(base + 1, sum_b)
            for row in chunks():
                at = slice(row, row + rows)
                dhid[at, :] += final(row)

        high, low = split(dhid[0:pixels, :])
        wide = mm(x80[:, 0:pixels], high)
        gin_ref[...] += wide[0:80] + wide[80:160] + mm(x80[0:80, 0:pixels], low)

    def big_image(index, carry):
        run(index, big_ref, big_noise_ref, index, SIDE, False)
        return carry

    lax.fori_loop(0, bigs, big_image, 0)

    def small_image(index, carry):
        run(bigs + index, small_ref, small_noise_ref, index, SMALL_SIDE, True)
        return carry

    lax.fori_loop(0, smalls, small_image, 0)

    emb = emb_ref[...].astype(F32)
    mine = jnp.concatenate(
        [emb[2 * k + 1 : 2 * k + 2] for k in range(count)] + [jnp.zeros((gtime.shape[1] - count, CH), F32)], axis=0
    ).astype(BF16)
    for number in range(2):
        time_g[number] = mm_tn(gtime[number].astype(BF16), mine)

    def out_copy(source, index):
        return pltpu.make_async_copy(source, grads_ref.at[owner_ref[index]], sem)

    for m in range(4):
        for j in range(2):
            part = slice(j * BLOCK, (j + 1) * BLOCK)
            for i in range(18):
                conv_w[m, i * BLOCK : (i + 1) * BLOCK, part] = conv_g[m, part, i * BLOCK : (i + 1) * BLOCK].astype(BF16)
    for number in range(2):
        for k in range(TIME_COUNT):
            i, j = k // 4, k % 4
            time_w[number, i * BLOCK : (i + 1) * BLOCK, j * BLOCK : (j + 1) * BLOCK] = time_g[
                number, j * BLOCK : (j + 1) * BLOCK, i * BLOCK : (i + 1) * BLOCK
            ].astype(BF16)
    for k in range(TRIPLE_COUNT):
        i, j = k // 6, k % 6
        triple_w[i * BLOCK : (i + 1) * BLOCK, j * BLOCK : (j + 1) * BLOCK] = triple_g[
            j * BLOCK : (j + 1) * BLOCK, i * BLOCK : (i + 1) * BLOCK
        ].astype(BF16)
    for k in range(PROJ_COUNT):
        i, j = k // 2, k % 2
        proj_w[i * BLOCK : (i + 1) * BLOCK, j * BLOCK : (j + 1) * BLOCK] = proj_g[
            j * BLOCK : (j + 1) * BLOCK, i * BLOCK : (i + 1) * BLOCK
        ].astype(BF16)

    def store_conv(index, carry):
        out_copy(conv_target(conv_w, index), index).start()
        return carry

    lax.fori_loop(0, 4 * CONV_BLOCKS, store_conv, 0)
    for index, target in others:
        out_copy(target, index).start()

    def wait_store(index, carry):
        out_copy(conv_target(conv_w, index), 0).wait()
        return carry

    lax.fori_loop(0, 4 * CONV_BLOCKS, wait_store, 0)
    for index, target in others:
        out_copy(target, index).wait()


def network_grads(owner_map, scalars, embed, big, big_noise, small, small_noise, mask, vectors, vin, head, whole):
    nb = owner_map.shape[0]
    slots = whole.shape[0]
    vmem = pl.BlockSpec(memory_space=pltpu.VMEM)
    smem = pl.BlockSpec(memory_space=pltpu.SMEM)
    hbm = pl.BlockSpec(memory_space=ANY)
    big_px = SIDE * SIDE
    tall = (SIDE + 2) * SIDE
    return pl.pallas_call(
        net_kernel,
        out_shape=(
            jax.ShapeDtypeStruct((slots, BLOCK, BLOCK), BF16),
            jax.ShapeDtypeStruct((80, CH), F32),
            jax.ShapeDtypeStruct((80, CH), F32),
            jax.ShapeDtypeStruct((80, CH), F32),
            jax.ShapeDtypeStruct((8, 128), F32),
        ),
        in_specs=[smem, smem] + [vmem] * 9 + [hbm],
        out_specs=(hbm, vmem, vmem, vmem, vmem),
        scratch_shapes=[
            pltpu.VMEM((4, 9 * CH, CH), BF16),
            pltpu.VMEM((2, CH, 2 * CH), BF16),
            pltpu.VMEM((CH, 3 * CH), BF16),
            pltpu.VMEM((CH, CH), BF16),
            pltpu.VMEM((4, CH, 9 * CH), F32),
            pltpu.VMEM((2, 2 * CH, CH), F32),
            pltpu.VMEM((3 * CH, CH), F32),
            pltpu.VMEM((CH, CH), F32),
            pltpu.VMEM((big_px, 2 * big_px), BF16),
            pltpu.VMEM((big_px, CH), F32),
            pltpu.VMEM((4, big_px, CH), F32),
            pltpu.VMEM((big_px, CH), F32),
            pltpu.VMEM((2, big_px, CH), F32),
            pltpu.VMEM((tall, 3 * CH), BF16),
            pltpu.VMEM((4, tall, 3 * CH), BF16),
            pltpu.VMEM((tall, 3 * CH), BF16),
            pltpu.VMEM((3, CH, big_px), BF16),
            pltpu.VMEM((big_px, big_px), F32),
            pltpu.VMEM((3, big_px, CH), BF16),
            pltpu.VMEM((2, CH, big_px), BF16),
            pltpu.VMEM((big_px, CH), BF16),
            pltpu.VMEM((big_px, CH), BF16),
            pltpu.VMEM((big_px, CH), BF16),
            pltpu.VMEM((big_px, CH), BF16),
            pltpu.VMEM((big_px, CH), F32),
            pltpu.VMEM((big_px, CH), F32),
            pltpu.VMEM((big_px, 3 * CH), BF16),
            pltpu.VMEM((2, embed.shape[0], 2 * CH), F32),
            pltpu.VMEM((2, 16, 2 * CH), F32),
            pltpu.VMEM((160, big_px), BF16),
            pltpu.SemaphoreType.DMA,
        ],
        compiler_params=pltpu.CompilerParams(vmem_limit_bytes=60 * 1024 * 1024),
        cost_estimate=pl.CostEstimate(flops=57 * 10**9, bytes_accessed=20 * 10**6, transcendentals=10**7),
    )(owner_map, scalars, embed, big, big_noise, small, small_noise, mask, vectors, vin, head, whole)


def sigma_of(levels):
    lowest = SIGMA_MIN ** (1.0 / RHO)
    highest = SIGMA_MAX ** (1.0 / RHO)
    return (lowest + levels.astype(F32) / (NSTEPS - 1) * (highest - lowest)) ** RHO


def shampoo(grads, master, moments, left_stats, right_stats, left_roots, right_roots):
    first = BETA_ONE * moments + (1 - BETA_ONE) * jnp.swapaxes(grads, 1, 2)
    left = BETA_TWO * left_stats + (1 - BETA_TWO) * jnp.einsum(
        "sji,sjk->sik", grads, grads, precision=HIGH
    )
    right = BETA_TWO * right_stats + (1 - BETA_TWO) * jnp.einsum(
        "sij,skj->sik", grads, grads, precision=HIGH
    )
    turned = jnp.einsum("sij,sjk->sik", left_roots, first, precision=HIGH)
    turned = jnp.einsum("sij,sjk->sik", turned, right_roots, precision=HIGH)
    norm_rms = jnp.sqrt(jnp.mean(turned * turned, axis=(1, 2), keepdims=True) + 1e-20)
    return (master - RATE_MATRIX * (turned / norm_rms + DECAY * master), first, left, right)


def adamw(grads, params, first, second):
    first = BETA_ONE * first + (1 - BETA_ONE) * grads
    second = BETA_TWO * second + (1 - BETA_TWO) * grads * grads
    fixed_first = first / (1 - BETA_ONE**STEP)
    fixed_second = second / (1 - BETA_TWO**STEP)
    return (
        params - RATE_VECTOR * (fixed_first / (jnp.sqrt(fixed_second) + 1e-08) + DECAY * params),
        first,
        second,
    )


def prepare(big_images, big_noise, small_images, small_noise, big_level, small_level, small_mask, vectors, pair_index):
    def half(values):
        count = values.shape[0] // 2
        return lax.dynamic_slice_in_dim(values, pair_index * count, count, 0)

    def rows8(values):
        return jnp.pad(values, ((0, 0), (0, 5), (0, 0)))

    levels = jnp.concatenate([half(big_level), half(small_level)])
    count = levels.shape[0]
    sigma = sigma_of(levels[:, None] + jnp.arange(2)[None, :])
    scale_in = lax.rsqrt(sigma * sigma + SIGMA_DATA**2)
    skip = SIGMA_DATA**2 / ((sigma - SIGMA_MIN) ** 2 + SIGMA_DATA**2)
    outer = (sigma - SIGMA_MIN) * SIGMA_DATA * lax.rsqrt(SIGMA_DATA**2 + sigma * sigma)
    rate = 1.0 / (sigma[:, 1] - sigma[:, 0])
    per_pass = jnp.stack([sigma, scale_in, skip, outer], axis=-1).reshape(count, 8)
    scalars = jnp.concatenate([per_pass, jnp.pad(rate[:, None], ((0, 0), (0, 7)))], axis=1).reshape(-1)
    half_ch = CH // 2
    freqs = jnp.exp(jnp.arange(half_ch, dtype=F32) * (math.log(100.0) / (half_ch - 1)))
    phase = (jnp.log(sigma) / 4.0).reshape(-1, 1) * freqs
    embed = jnp.concatenate([jnp.sin(phase), jnp.cos(phase)], axis=-1)
    embed = jnp.pad(embed, ((0, -embed.shape[0] % 16), (0, 0))).astype(BF16)
    vin = jnp.pad(vectors[0:27].reshape(9, 3, CH), ((0, 0), (0, 5), (0, 0))).reshape(72, CH)
    vin = jnp.concatenate([vin, vectors[27:28], jnp.zeros((7, CH), F32)], axis=0)
    head = jnp.pad(vectors[47:74].reshape(9, 3, CH), ((0, 0), (0, 5), (0, 0))).reshape(72, CH)
    head = jnp.pad(head, ((0, 8), (0, 0)))
    mask = jnp.broadcast_to(half(small_mask).astype(F32)[:, None, :], (small_mask.shape[0] // 2, 8, small_mask.shape[1]))
    return (
        scalars,
        embed,
        rows8(half(big_images)),
        rows8(half(big_noise)),
        rows8(half(small_images)),
        rows8(half(small_noise)),
        mask,
        jnp.pad(vectors, ((0, 6), (0, 0))),
        vin,
        head,
    )


def local(
    big_images,
    big_noise,
    small_images,
    small_noise,
    big_level,
    small_level,
    small_mask,
    owner_map,
    blocks,
    moments,
    left_stats,
    right_stats,
    left_roots,
    right_roots,
    vectors,
    vec_first,
    vec_second,
):
    slot_count = blocks.shape[0]
    whole = lax.all_gather(blocks.astype(BF16), ("pair", "dp"), axis=0, tiled=True)
    ready = prepare(
        big_images, big_noise, small_images, small_noise, big_level, small_level, small_mask, vectors, lax.axis_index("pair")
    )
    grads, gvec, gin, ghead, loss = network_grads(owner_map, *ready, whole)
    summed = lax.psum_scatter(grads.reshape(grads.shape[0], -1), ("pair", "dp"), scatter_dimension=0, tiled=True)
    slot_ids = lax.axis_index(("pair", "dp")) * slot_count + jnp.arange(slot_count, dtype=jnp.int32)
    owned = jnp.any(slot_ids[:, None] == owner_map[None, :], axis=1)
    mine = jnp.where(owned[:, None], summed.astype(F32), 0.0)
    vec_part = jnp.concatenate(
        [
            gin[0:72].reshape(9, 8, CH)[:, 0:3].reshape(27, CH),
            gin[72:73],
            gvec[28:47],
            ghead[0:72].reshape(9, 8, CH)[:, 0:3].reshape(27, CH),
        ],
        axis=0,
    )
    vec_total, loss_total, square = lax.psum((vec_part, loss[0, 0], jnp.sum(mine * mine)), ("pair", "dp"))
    grad_norm = jnp.sqrt(square + jnp.sum(vec_total * vec_total))
    factor = jnp.minimum(1.0, CLIP / (grad_norm + 1e-06))
    slot_grad = mine.reshape(blocks.shape) * factor
    new_blocks, new_moments, new_left, new_right = shampoo(
        slot_grad, blocks, moments, left_stats, right_stats, left_roots, right_roots
    )
    new_vectors, new_first, new_second = adamw(vec_total * factor, vectors, vec_first, vec_second)
    return (
        loss_total,
        grad_norm,
        new_blocks,
        new_moments,
        new_left,
        new_right,
        new_vectors,
        new_first,
        new_second,
    )


def solution(mesh):
    by_slot = P(("pair", "dp"), None, None)
    by_image = P("dp", None, None)
    placed = (by_image,) * 4 + (P("dp"), P("dp"), P("dp", None), P()) + (by_slot,) * 6 + (P(),) * 3
    return jax.shard_map(
        local,
        mesh=mesh,
        in_specs=placed,
        out_specs=(P(), P()) + (by_slot,) * 4 + (P(),) * 3,
        check_vma=False,
    )
```

time: 1290 us -> 592 us (0.46)
  local copies, waits for them, and re-layouts: 471 us -> 50 us
  matrix products: 295 us -> 7.77 us
  other arithmetic: 239 us -> 12.8 us
  Pallas kernels: 12.8 us -> 126 us
  blocking collectives: 42.2 us -> 135 us
  starting transfers between devices: 3.62 us -> 60.5 us
  between operations: 32.5 us -> 17.1 us
    dot_general x86 -> x0, matrix products: 283 us -> none  [the longest x37 97.8 us: product_plain(): jnp.dot(left.astype(jnp.bfloat16), right.astype(jnp.bfloat16), preferred_...]
    pallas_call x0 -> x1, Pallas kernels: none -> 126 us  [network_grads(): pl.pallas_call(net_kernel, out_shape=(jax.ShapeDtypeStruct((slots, BLOCK,...]
    unnamed x1012 -> x33, local copies, waits for them, and re-layouts: 147 us -> 36.7 us
    reduce_sum x132 -> x2, other arithmetic: 105 us -> 2.32 us  [the longest x1 1.51 us: local(): grad_norm = jnp.sqrt(square + jnp.sum(vec_total * vec_total))]
    unnamed x0 -> x1, blocking collectives: none -> 92.5 us
    dot_general x20 -> x0, local copies, waits for them, and re-layouts: 86.8 us -> none  [the longest x17 64.6 us: product_low(): return rounded_product(left, right)]
    psum x1, waiting for transfers between devices: 182 us -> 113 us  [local(): lax.psum((vec_part, loss[0, 0], jnp.sum(mine * mine)), ('pair', 'dp'))]
    all_gather x1, waiting for transfers between devices: 0.02 us -> 60.8 us  [local(): lax.all_gather(blocks.astype(BF16), ('pair', 'dp'), axis=0, tiled=True)]
  transfers between devices with their start and end apart: 4 -> 10, of which waited for: 1 -> 3; matrix products, arithmetic and copies ran while one was open for 22% -> 3% of each run, Pallas kernels for 0% -> 0%
where the time goes in v1:
time: 592 us; the launch traced here: 588 us
  waiting for transfers between devices  179 us (30%)
  blocking collectives  135 us (23%)
  Pallas kernels  126 us (21%)
  starting transfers between devices  60.5 us (10%)
  local copies, waits for them, and re-layouts  50 us (8%)
  between operations  17.1 us (3%)
  other arithmetic  12.8 us (2%)
  matrix products  7.77 us (1%)
    pallas_call x1, Pallas kernels, network_grads(): pl.pallas_call(net_kernel, out_shape=(jax.ShapeDtypeStruct((slots, BLOCK,...  126 us
    psum x1, waiting for transfers between devices, local(): lax.psum((vec_part, loss[0, 0], jnp.sum(mine * mine)), ('pair', 'dp'))  113 us
    unnamed x1, blocking collectives  92.5 us
    all_gather x1, waiting for transfers between devices, local(): lax.all_gather(blocks.astype(BF16), ('pair', 'dp'), axis=0, tiled=True)  60.8 us
    unnamed x8, starting transfers between devices  60.5 us
    psum x1, blocking collectives, local(): lax.psum((vec_part, loss[0, 0], jnp.sum(mine * mine)), ('pair', 'dp'))  42.6 us
    unnamed x33, local copies, waits for them, and re-layouts  36.7 us
  transfers between devices with their start and end apart: 10, of which 3 were waited for; matrix products, arithmetic and copies ran while one was open for 3% of the time, Pallas kernels for 0%

profile of v1, /device:TPU:0, one launch (start us, length us, event | category | flops | bytes accessed | tf_op | source)
XLA Modules:
  0.0 587.9 jit_solution(12111049907669446370)
XLA Ops:
  7.2 1.7 convert_element_type.59
  9.1 0.7 dynamic_slice.21
  9.8 1.2 dynamic_slice.22
  11.0 0.7 pad_add_fusion
  11.8 0.1 copy.56
  11.9 0.1 reshape.241
  12.0 0.1 log_multiply_fusion
  12.0 0.1 subtract_divide_fusion
  12.1 0.1 select_maximum_fusion
  12.2 0.6 reshape.242.scal_ref
  12.8 0.1 reshape.255
  12.9 0.8 constant_dynamic-slice_fusion.3
  13.8 0.7 slice.39
  14.5 1.5 pad.44.vec_ref
  16.0 0.6 pad.40.big_ref
  16.6 0.6 pad.41.big_noise_ref
  17.3 0.7 constant_dynamic-slice_fusion.1
  18.0 0.6 pad.42.small_ref
  18.6 0.6 pad.43.small_noise_ref
  19.2 0.8 fusion.18
  20.0 0.6 pad.47.head_ref
  20.7 0.1 pad.54.clone
  20.8 0.7 fusion.16
  21.5 0.1 fusion.13
  21.6 0.6 fusion.12.emb_ref
  22.2 0.7 maximum_maximum_fusion.vin_ref
  22.9 60.8 %all-gather.2.cloned.1.call-done.whole_ref = bf16[192,128,128]{2,1,0:T(8,128)(2,1)} async-done(((bf16[6,128,128]{2,1,0:T(8,128)(2,1)}), bf16[192,128,128]{2,1,0:T(8,128)(2,1)}) %all-gather.2.cloned.1.call-update) | async-done | bytes 6291472 | tf_op jit(solution)/shard_map/all_gather | solution.py:768
  83.7 0.6 broadcast_in_dim.15.mask_ref
  84.3 125.8 %shard_map.232 = (bf16[192,128,128]{2,1,0:T(8,128)(2,1)}, f32[80,256]{1,0:T(8,128)}, f32[80,256]{1,0:T(8,128)}, f32[80,256]{1,0:T(8,128)}, f32[8,128]{1,0:T(8,128)}) custom-call(s32[176]{0:T(256)} %owner_ref.1, f32[48]{0:T(128)} %reshape.242.scal_ref, bf16[16,256]{1,0:T(8,128)(2,1)} %fusion.12.emb_ref, f32[2,8,1024]{2,1,0:T(8,128)} %pad.40.big_ref, ...), custom_call_target="tpu_custom_call" | custom-call | flops 57000001536 | bytes 20000000 | tf_op jit(solution)/shard_map/pallas_call | solution.py:626
  210.1 11.2 %copy.83 = bf16[24,8,128,128]{3,1,2,0:T(8,128)(2,1)} copy(bf16[24,8,128,128]{3,2,1,0:T(8,128)(2,1)} %bitcast.35) | data formatting | bytes 12582912
  221.3 92.5 %fusion = bf16[8,16384]{1,0:T(8,128)(2,1)S(1)} fusion(bf16[192,16384]{1,0:T(8,128)(2,1)} %bitcast.34), kind=kCustom, calls=%all-reduce-scatter | all-reduce-scatter fusion | flops 4194305 | bytes 6553600
  313.8 3.2 collective-permute-start
  317.0 4.2 collective-permute-start.1
  321.2 0.1 slice.50
  321.3 6.0 %collective-permute-start.2 = (bf16[8,16384]{1,0:T(8,128)(2,1)S(1)}, bf16[8,16384]{1,0:T(8,128)(2,1)S(1)}, u32[]{:S(2)}, u32[]{:S(2)}) collective-permute-start(bf16[8,16384]{1,0:T(8,128)(2,1)S(1)} %fusion), channel_id=1, source_target_pairs={{0,3},{1,4},{2,5},{3,6},{4,7},{5,8},{6,9},{7,10},{8,11},{9,12},{10... | collective-permute-start | bytes 786440
  327.3 1.9 collective-permute-start.3
  329.2 6.4 %collective-permute-start.7 = (bf16[6,16384]{1,0:T(8,128)(2,1)S(1)}, bf16[6,16384]{1,0:T(8,128)(2,1)S(1)}, u32[]{:S(2)}, u32[]{:S(2)}) collective-permute-start(bf16[6,16384]{1,0:T(8,128)(2,1)S(1)} %slice.50), channel_id=1, source_target_pairs={{0,8},{1,9},{2,10},{3,11},{4,12},{5,13},{6,14},{7,15},{8,16},{9,17... | collective-permute-start | bytes 589832
  335.7 0.8 slice.45
  336.4 4.5 collective-permute-done.7
  341.0 7.8 %collective-permute-start.4 = (bf16[8,16384]{1,0:T(8,128)(2,1)S(1)}, bf16[8,16384]{1,0:T(8,128)(2,1)S(1)}, u32[]{:S(2)}, u32[]{:S(2)}) collective-permute-start(bf16[8,16384]{1,0:T(8,128)(2,1)S(1)} %fusion), channel_id=1, source_target_pairs={{0,5},{1,6},{2,7},{3,8},{4,9},{5,10},{6,11},{7,12},{8,13},{9,14},{... | collective-permute-start | bytes 786440
  348.8 22.6 %collective-permute-start.5 = (bf16[8,16384]{1,0:T(8,128)(2,1)S(1)}, bf16[8,16384]{1,0:T(8,128)(2,1)S(1)}, u32[]{:S(2)}, u32[]{:S(2)}) collective-permute-start(bf16[8,16384]{1,0:T(8,128)(2,1)S(1)} %fusion), channel_id=1, source_target_pairs={{0,6},{1,7},{2,8},{3,9},{4,10},{5,11},{6,12},{7,13},{8,14},{9,15},... | collective-permute-start | bytes 786440
  371.4 8.4 %collective-permute-start.6 = (bf16[8,16384]{1,0:T(8,128)(2,1)S(1)}, bf16[8,16384]{1,0:T(8,128)(2,1)}, u32[]{:S(2)}, u32[]{:S(2)}) collective-permute-start(bf16[8,16384]{1,0:T(8,128)(2,1)S(1)} %fusion), channel_id=1, source_target_pairs={{0,7},{1,8},{2,9},{3,10},{4,11},{5,12},{6,13},{7,14},{8,15},{9,16}... | collective-permute-start | bytes 786440
  379.8 0.6 pad_maximum_fusion
  380.5 0.2 compare_reduce_fusion
  380.7 0.9 copy.61
  381.6 1.2 slice.41
  382.8 113.4 %all-reduce.15.cloned.1.call-done = f32[74,256]{1,0:T(8,128)} async-done(((f32[74,256]{1,0:T(8,128)}), f32[74,256]{1,0:T(8,128)}) %all-reduce.15.cloned.1.call-update) | async-done | bytes 75792 | tf_op jit(solution)/shard_map/psum | solution.py:786
  496.2 1.5 multiply_reduce_fusion.2
  497.8 0.7 copy-done.2
  498.4 0.1 copy-done.3
  498.5 0.1 copy-done.5
  498.6 0.7 copy-done.6
  499.3 22.1 %concatenate.21 = bf16[70,16384]{1,0:T(8,128)(2,1)S(1)} concatenate(bf16[6,16384]{1,0:T(8,128)(2,1)} %copy-done.4, bf16[8,16384]{1,0:T(8,128)(2,1)} %collective-permute-done.6, bf16[8,16384]{1,0:T(8,128)(2,1)} %copy-done.6, bf16[8,16384]{1,0:T(8,128)(2,1)} %copy-done.5, bf16[8,16384]{1,0:T(8,128)(2,1)} %copy-done.3, bf16[8,16384]{1,0:T(8,128)(2,1)} %copy-done.2, ...), dimensions={0} | concatenate | bytes 4587520
  521.4 0.8 multiply_reduce_fusion
  522.2 42.6 %all-reduce.12 = (f32[]{:T(128)}, f32[]{:T(128)}) all-reduce(f32[]{:T(128)} %bitcast.3, f32[]{:T(128)} %multiply_reduce_fusion), channel_id=1, replica_groups=mesh['pair'=2,'dp'=16] {'pair','dp'}, use_global_device_ids=true, to_apply=%region_0.1 | all-reduce | flops 2 | bytes 16 | tf_op jit(solution)/shard_map/psum | solution.py:786
  566.1 0.1 multiply_bitcast_fusion
  566.3 1.1 fusion.6
  567.4 0.9 copy.64
  568.4 1.9 fusion.19
  570.3 0.6 multiply_reduce_fusion.1
  570.9 2.7 fusion.1
  573.6 2.6 fusion.2
  576.2 1.9 multiply_subtract_fusion
  578.1 1.6 multiply_subtract_fusion.1
  (52 shorter events, 0.4 us)
Async XLA Ops:
  7.2 563.1 %copy-start = (f32[6,128,128]{2,1,0:T(8,128)S(1)}, f32[6,128,128]{2,1,0:T(8,128)}, u32[]{:S(2)}) copy-start(f32[6,128,128]{2,1,0:T(8,128)} %param.30) | copy-start | bytes 1179652
  7.2 76.5 %all-gather.2.cloned.1.call-start = ((), (), s32[]{:S(2)}) async-start(), calls=%async_computation | async-start | bytes 6488064 | tf_op jit(solution)/shard_map/all_gather | solution.py:768
  9.0 487.2 %all-reduce.15.cloned.1.call-start = ((), (), s32[]{:S(2)}) async-start(), calls=%async_computation.1 | async-start | bytes 163840 | tf_op jit(solution)/shard_map/psum | solution.py:786
  221.3 99.9 %copy-start.9 = (f32[80,256]{1,0:T(8,128)S(1)}, f32[80,256]{1,0:T(8,128)}, u32[]{:S(2)}) copy-start(f32[80,256]{1,0:T(8,128)} %get-tuple-element.16) | copy-start | bytes 245764
  221.3 114.4 %copy-start.10 = (f32[80,256]{1,0:T(8,128)S(1)}, f32[80,256]{1,0:T(8,128)}, u32[]{:S(2)}) copy-start(f32[80,256]{1,0:T(8,128)} %get-tuple-element.18) | copy-start | bytes 245764
  221.3 159.2 %copy-start.11 = (s32[176]{0:T(256)S(1)}, s32[176]{0:T(256)}, u32[]{:S(2)}) copy-start(s32[176]{0:T(256)} %owner_ref.1) | copy-start | bytes 2116
  221.3 159.4 %copy-start.1 = (f32[6,128,128]{2,1,0:T(8,128)S(1)}, f32[6,128,128]{2,1,0:T(8,128)}, u32[]{:S(2)}) copy-start(f32[6,128,128]{2,1,0:T(8,128)} %param.26) | copy-start | bytes 1179652
  313.8 35.0 %collective-permute-start = (bf16[8,16384]{1,0:T(8,128)(2,1)S(1)}, bf16[8,16384]{1,0:T(8,128)(2,1)S(1)}, u32[]{:S(2)}, u32[]{:S(2)}) collective-permute-start(bf16[8,16384]{1,0:T(8,128)(2,1)S(1)} %fusion), channel_id=1, source_target_pairs={{0,1},{1,2},{2,3},{3,4},{4,5},{5,6},{6,7},{7,8},{8,9},{9,10},{10,1... | collective-permute-start | bytes 786440
  317.0 54.4 %collective-permute-start.1 = (bf16[8,16384]{1,0:T(8,128)(2,1)S(1)}, bf16[8,16384]{1,0:T(8,128)(2,1)S(1)}, u32[]{:S(2)}, u32[]{:S(2)}) collective-permute-start(bf16[8,16384]{1,0:T(8,128)(2,1)S(1)} %fusion), channel_id=1, source_target_pairs={{0,2},{1,3},{2,4},{3,5},{4,6},{5,7},{6,8},{7,9},{8,10},{9,11},{10,... | collective-permute-start | bytes 786440
  321.3 176.4 %collective-permute-start.2 = (bf16[8,16384]{1,0:T(8,128)(2,1)S(1)}, bf16[8,16384]{1,0:T(8,128)(2,1)S(1)}, u32[]{:S(2)}, u32[]{:S(2)}) collective-permute-start(bf16[8,16384]{1,0:T(8,128)(2,1)S(1)} %fusion), channel_id=1, source_target_pairs={{0,3},{1,4},{2,5},{3,6},{4,7},{5,8},{6,9},{7,10},{8,11},{9,12},{10... | collective-permute-start | bytes 786440
  327.3 170.4 %collective-permute-start.3 = (bf16[8,16384]{1,0:T(8,128)(2,1)S(1)}, bf16[8,16384]{1,0:T(8,128)(2,1)S(1)}, u32[]{:S(2)}, u32[]{:S(2)}) collective-permute-start(bf16[8,16384]{1,0:T(8,128)(2,1)S(1)} %fusion), channel_id=1, source_target_pairs={{0,4},{1,5},{2,6},{3,7},{4,8},{5,9},{6,10},{7,11},{8,12},{9,13},{1... | collective-permute-start | bytes 786440
  329.2 11.7 %collective-permute-start.7 = (bf16[6,16384]{1,0:T(8,128)(2,1)S(1)}, bf16[6,16384]{1,0:T(8,128)(2,1)S(1)}, u32[]{:S(2)}, u32[]{:S(2)}) collective-permute-start(bf16[6,16384]{1,0:T(8,128)(2,1)S(1)} %slice.50), channel_id=1, source_target_pairs={{0,8},{1,9},{2,10},{3,11},{4,12},{5,13},{6,14},{7,15},{8,16},{9,17... | collective-permute-start | bytes 589832
  341.0 156.8 %copy-start.4 = (bf16[6,16384]{1,0:T(8,128)(2,1)}, bf16[6,16384]{1,0:T(8,128)(2,1)S(1)}, u32[]{:S(2)}) copy-start(bf16[6,16384]{1,0:T(8,128)(2,1)S(1)} %collective-permute-done.7) | copy-start | bytes 589828
  341.0 156.8 %collective-permute-start.4 = (bf16[8,16384]{1,0:T(8,128)(2,1)S(1)}, bf16[8,16384]{1,0:T(8,128)(2,1)S(1)}, u32[]{:S(2)}, u32[]{:S(2)}) collective-permute-start(bf16[8,16384]{1,0:T(8,128)(2,1)S(1)} %fusion), channel_id=1, source_target_pairs={{0,5},{1,6},{2,7},{3,8},{4,9},{5,10},{6,11},{7,12},{8,13},{9,14},{... | collective-permute-start | bytes 786440
  348.8 149.0 %collective-permute-start.5 = (bf16[8,16384]{1,0:T(8,128)(2,1)S(1)}, bf16[8,16384]{1,0:T(8,128)(2,1)S(1)}, u32[]{:S(2)}, u32[]{:S(2)}) collective-permute-start(bf16[8,16384]{1,0:T(8,128)(2,1)S(1)} %fusion), channel_id=1, source_target_pairs={{0,6},{1,7},{2,8},{3,9},{4,10},{5,11},{6,12},{7,13},{8,14},{9,15},... | collective-permute-start | bytes 786440
  371.4 127.9 %collective-permute-start.6 = (bf16[8,16384]{1,0:T(8,128)(2,1)S(1)}, bf16[8,16384]{1,0:T(8,128)(2,1)}, u32[]{:S(2)}, u32[]{:S(2)}) collective-permute-start(bf16[8,16384]{1,0:T(8,128)(2,1)S(1)} %fusion), channel_id=1, source_target_pairs={{0,7},{1,8},{2,9},{3,10},{4,11},{5,12},{6,13},{7,14},{8,15},{9,16}... | collective-permute-start | bytes 786440
  497.7 0.7 copy-start.2
  497.7 0.8 copy-start.3
  497.7 0.9 copy-start.5
  498.6 0.7 copy-start.6
  566.3 11.8 %copy-start.7 = (f32[74,256]{1,0:T(8,128)S(1)}, f32[74,256]{1,0:T(8,128)}, u32[]{:S(2)}) copy-start(f32[74,256]{1,0:T(8,128)} %param.32) | copy-start | bytes 227332
  566.3 11.8 %copy-start.8 = (f32[74,256]{1,0:T(8,128)S(1)}, f32[74,256]{1,0:T(8,128)}, u32[]{:S(2)}) copy-start(f32[74,256]{1,0:T(8,128)} %param.33) | copy-start | bytes 227332
Sparse Core Ops, SparseCore 0:
  11.5 72.2 all-gather.1
  380.6 115.5 all-reduce.14

commit v2 on v1

--- a/solution.py
+++ b/solution.py
@@ -141,9 +141,6 @@
     whole_ref,
     grads_ref,
     gvec_ref,
-    gin_ref,
-    ghead_ref,
-    loss_ref,
     conv_w,
     time_w,
     triple_w,
@@ -174,6 +171,9 @@
     tsh,
     gtime,
     x80,
+    gin_ref,
+    ghead_ref,
+    loss_ref,
     sem,
 ):
     bigs = big_ref.shape[0]
@@ -393,7 +393,7 @@
         total = jnp.sum(jnp.sum(weighted * diff, axis=1, keepdims=True), axis=0, keepdims=True)
         root = jnp.sqrt(total + bound * bound)
         rate = scal(2, 0)
-        loss_ref[...] += jnp.broadcast_to((root - bound) * rate, (8, 128))
+        loss_ref[...] += jnp.broadcast_to((root - bound) * rate, (8, CH))
         dout = weighted * ((rate * scal(1, 3)) / root)
 
         parts = []
@@ -573,6 +573,12 @@
     for number in range(2):
         time_g[number] = mm_tn(gtime[number].astype(BF16), mine)
 
+    for tap in range(9):
+        gvec_ref[3 * tap : 3 * tap + 3, :] = gin_ref[8 * tap : 8 * tap + 3, :]
+        gvec_ref[47 + 3 * tap : 50 + 3 * tap, :] = ghead_ref[8 * tap : 8 * tap + 3, :]
+    gvec_ref[27:28, :] = gin_ref[72:73, :]
+    gvec_ref[74:75, :] = loss_ref[0:1, :]
+
     def out_copy(source, index):
         return pltpu.make_async_copy(source, grads_ref.at[owner_ref[index]], sem)
 
@@ -628,12 +634,9 @@
         out_shape=(
             jax.ShapeDtypeStruct((slots, BLOCK, BLOCK), BF16),
             jax.ShapeDtypeStruct((80, CH), F32),
-            jax.ShapeDtypeStruct((80, CH), F32),
-            jax.ShapeDtypeStruct((80, CH), F32),
-            jax.ShapeDtypeStruct((8, 128), F32),
         ),
         in_specs=[smem, smem] + [vmem] * 9 + [hbm],
-        out_specs=(hbm, vmem, vmem, vmem, vmem),
+        out_specs=(hbm, vmem),
         scratch_shapes=[
             pltpu.VMEM((4, 9 * CH, CH), BF16),
             pltpu.VMEM((2, CH, 2 * CH), BF16),
@@ -665,11 +668,507 @@
             pltpu.VMEM((2, embed.shape[0], 2 * CH), F32),
             pltpu.VMEM((2, 16, 2 * CH), F32),
             pltpu.VMEM((160, big_px), BF16),
+            pltpu.VMEM((80, CH), F32),
+            pltpu.VMEM((80, CH), F32),
+            pltpu.VMEM((8, CH), F32),
             pltpu.SemaphoreType.DMA,
         ],
         compiler_params=pltpu.CompilerParams(vmem_limit_bytes=60 * 1024 * 1024),
         cost_estimate=pl.CostEstimate(flops=57 * 10**9, bytes_accessed=20 * 10**6, transcendentals=10**7),
     )(owner_map, scalars, embed, big, big_noise, small, small_noise, mask, vectors, vin, head, whole)
+
+
+MESH_ID = pl.DeviceIdType.MESH
+
+
+def where_am_i():
+    dp = lax.axis_index("dp")
+    return lax.axis_index("pair"), dp // 4, (dp // 2) % 2, dp % 2
+
+
+def device(pair, line, mid, core):
+    return (pair, (line * 2 + mid) * 2 + core)
+
+
+def neighbours():
+    pair, line, mid, core = where_am_i()
+    flip_pair, flip_mid = 1 - 2 * pair, 1 - 2 * mid
+    second = device(pair + (1 - core) * flip_pair, line, mid + core * flip_mid, core)
+    third = device(pair + core * flip_pair, line, mid + (1 - core) * flip_mid, core)
+    sibling = device(pair, line, mid, 1 - core)
+    at_second = (1 - core) * pair + core * mid
+    at_third = core * pair + (1 - core) * mid
+    return pair, line, mid, core, at_second, at_third, second, third, sibling
+
+
+def greet(lines, devices, lower, upper, line):
+    barrier = pltpu.get_barrier_semaphore()
+    for other in devices:
+        pl.semaphore_signal(barrier, inc=1, device_id=other, device_id_type=MESH_ID)
+    for there, other in ((lower >= 0, lower), (upper < lines, upper)):
+
+        @pl.when(there)
+        def _(other=other):
+            pl.semaphore_signal(barrier, inc=1, device_id=line(other), device_id_type=MESH_ID)
+
+    beside = jnp.where(lower >= 0, 1, 0) + jnp.where(upper < lines, 1, 0)
+    pl.semaphore_wait(barrier, len(devices) + beside)
+
+
+def gather_kernel(
+    lines, blocks_ref, whole_ref, own, up_send, down_send, second_send, third_send, sib_send, line_recv, second_recv, third_recv, sib_recv, own_sem
+):
+    pair, line, mid, core, at_second, at_third, second, third, sibling = neighbours()
+    count = blocks_ref.shape[0]
+    group = 4 * lines
+    upper = device(pair, line + 1, mid, core)
+    lower = device(pair, line - 1, mid, core)
+
+    def place(l, s, t, c):
+        p = (1 - c) * s + c * t
+        m = c * s + (1 - c) * t
+        return whole_ref.at[pl.ds((p * group + (l * 2 + m) * 2 + c) * count, count)]
+
+    def copy(source, target, send, recv, to):
+        return pltpu.make_async_remote_copy(
+            src_ref=source, dst_ref=target, send_sem=send, recv_sem=recv, device_id=to, device_id_type=MESH_ID
+        )
+
+    def to_sibling(l, s, t, source=None):
+        where = place(l, s, t, core)
+        p = (1 - core) * s + core * t
+        m = core * s + (1 - core) * t
+        index = l * 4 + p * 2 + m
+        return copy(where if source is None else source, where, sib_send.at[index], sib_recv.at[index], sibling)
+
+    def to_second(l, source=None):
+        where = place(l, at_second, at_third, core)
+        return copy(where if source is None else source, where, second_send.at[l], second_recv.at[l], second)
+
+    def to_third(l, s, source=None):
+        where = place(l, s, at_third, core)
+        index = l * 2 + s
+        return copy(where if source is None else source, where, third_send.at[index], third_recv.at[index], third)
+
+    def to_upper(l, source=None):
+        where = place(l, at_second, at_third, core)
+        return copy(where if source is None else source, where, up_send.at[l], line_recv.at[l], upper)
+
+    def to_lower(l, source=None):
+        where = place(l, at_second, at_third, core)
+        return copy(where if source is None else source, where, down_send.at[l], line_recv.at[l], lower)
+
+    own[...] = blocks_ref[...].astype(BF16)
+    greet(lines, (second, third, sibling), line - 1, line + 1, lambda l: device(pair, l, mid, core))
+
+    @pl.when(line < lines - 1)
+    def _():
+        to_upper(line, own).start()
+
+    @pl.when(line > 0)
+    def _():
+        to_lower(line, own).start()
+
+    to_third(line, at_second, own).start()
+    to_second(line, own).start()
+    to_sibling(line, at_second, at_third, own).start()
+    keep = pltpu.make_async_copy(own, place(line, at_second, at_third, core), own_sem)
+    keep.start()
+
+    def from_second(l):
+        to_second(l).wait_recv()
+        to_third(l, 1 - at_second).start()
+        to_sibling(l, 1 - at_second, at_third).start()
+
+    def from_line(l):
+        to_upper(l).wait_recv()
+
+        @pl.when((l < line) & (line < lines - 1))
+        def _():
+            to_upper(l).start()
+
+        @pl.when((l > line) & (line > 0))
+        def _():
+            to_lower(l).start()
+
+        to_second(l).start()
+        to_third(l, at_second).start()
+        to_sibling(l, at_second, at_third).start()
+
+    def both(distance, carry):
+        @pl.when(line - distance >= 0)
+        def _():
+            from_line(line - distance)
+
+        @pl.when(line + distance < lines)
+        def _():
+            from_line(line + distance)
+
+        @pl.when(line - distance + 1 >= 0)
+        def _():
+            from_second(line - distance + 1)
+
+        @pl.when((line + distance - 1 < lines) & (distance > 1))
+        def _():
+            from_second(line + distance - 1)
+
+        return carry
+
+    lax.fori_loop(1, lines + 1, both, 0)
+
+    def from_third(l, carry):
+        for s in range(2):
+            to_third(l, s).wait_recv()
+            to_sibling(l, s, 1 - at_third).start()
+        return carry
+
+    lax.fori_loop(0, lines, from_third, 0)
+
+    def finish(l, carry):
+        @pl.when((l <= line) & (line < lines - 1))
+        def _():
+            to_upper(l).wait_send()
+
+        @pl.when((l >= line) & (line > 0))
+        def _():
+            to_lower(l).wait_send()
+
+        to_second(l).wait_send()
+        for s in range(2):
+            to_third(l, s).wait_send()
+            for t in range(2):
+                done = to_sibling(l, s, t)
+                done.wait_send()
+                done.wait_recv()
+        return carry
+
+    lax.fori_loop(0, lines, finish, 0)
+    keep.wait()
+
+
+def gather_blocks(blocks):
+    lines = lax.axis_size("dp") // 4
+    count = blocks.shape[0]
+    total = count * lines * 8
+    dma = pltpu.SemaphoreType.DMA
+    return pl.pallas_call(
+        partial(gather_kernel, lines),
+        out_shape=jax.ShapeDtypeStruct((total, BLOCK, BLOCK), BF16),
+        in_specs=[pl.BlockSpec(memory_space=pltpu.VMEM)],
+        out_specs=pl.BlockSpec(memory_space=ANY),
+        scratch_shapes=[
+            pltpu.VMEM((count, BLOCK, BLOCK), BF16),
+            dma((lines,)),
+            dma((lines,)),
+            dma((lines,)),
+            dma((2 * lines,)),
+            dma((4 * lines,)),
+            dma((lines,)),
+            dma((lines,)),
+            dma((2 * lines,)),
+            dma((4 * lines,)),
+            dma,
+        ],
+        compiler_params=pltpu.CompilerParams(collective_id=0, has_side_effects=True),
+        cost_estimate=pl.CostEstimate(flops=0, bytes_accessed=2 * total * BLOCK * BLOCK * 2, transcendentals=0),
+    )(blocks)
+
+
+def sum_kernel(
+    lines,
+    grads_ref,
+    vec_in,
+    owned_ref,
+    sum_ref,
+    vec_ref,
+    square_ref,
+    mine,
+    from_sib,
+    from_third,
+    from_second,
+    from_lower,
+    from_upper,
+    vec_own,
+    vec_got,
+    sq_own,
+    sq_got,
+    load_sem,
+    sib_send,
+    third_send,
+    second_send,
+    up_send,
+    down_send,
+    sib_recv,
+    third_recv,
+    second_recv,
+    up_recv,
+    down_recv,
+    vec_send,
+    vec_recv,
+    sq_send,
+    sq_recv,
+):
+    pair, line, mid, core, at_second, at_third, second, third, sibling = neighbours()
+    count = sum_ref.shape[0]
+    group = 4 * lines
+    upper = device(pair, line + 1, mid, core)
+    lower = device(pair, line - 1, mid, core)
+    steps = lines.bit_length() - 1
+    hops = [sibling, third, second]
+    far = []
+    for bit in range(steps):
+        flipped = line + (1 - 2 * ((line // 2**bit) % 2)) * 2**bit
+        far.append(device(pair, flipped, mid, core))
+
+    def copy(source, target, send, recv, to):
+        return pltpu.make_async_remote_copy(
+            src_ref=source, dst_ref=target, send_sem=send, recv_sem=recv, device_id=to, device_id_type=MESH_ID
+        )
+
+    def spot(l, s, t):
+        return l * 4 + s * 2 + t
+
+    def slots(l, s, t, c):
+        p = (1 - c) * s + c * t
+        m = c * s + (1 - c) * t
+        return pl.ds((p * group + (l * 2 + m) * 2 + c) * count, count)
+
+    def to_sibling(l, s, t):
+        index = spot(l, s, t)
+        return copy(grads_ref.at[slots(l, s, t, 1 - core)], from_sib.at[index], sib_send.at[index], sib_recv.at[index], sibling)
+
+    def load(l, s, t):
+        index = spot(l, s, t)
+        return pltpu.make_async_copy(grads_ref.at[slots(l, s, t, core)], mine.at[index], load_sem.at[index])
+
+    def to_third(l, s):
+        index = l * 2 + s
+        return copy(mine.at[spot(l, s, 1 - at_third)], from_third.at[index], third_send.at[index], third_recv.at[index], third)
+
+    def to_second(l):
+        return copy(mine.at[spot(l, 1 - at_second, at_third)], from_second.at[l], second_send.at[l], second_recv.at[l], second)
+
+    def to_upper(l):
+        return copy(mine.at[spot(l, at_second, at_third)], from_lower.at[l], up_send.at[l], up_recv.at[l], upper)
+
+    def to_lower(l):
+        return copy(mine.at[spot(l, at_second, at_third)], from_upper.at[l], down_send.at[l], down_recv.at[l], lower)
+
+    def vec_step(k):
+        to = (hops + far)[k]
+        return copy(vec_own.at[k], vec_got.at[k], vec_send.at[k], vec_recv.at[k], to)
+
+    def vec_next(k):
+        vec_step(k).wait_recv()
+        if k < 2 + steps:
+            vec_own[k + 1] = vec_own[k] + vec_got[k]
+            vec_step(k + 1).start()
+        else:
+            vec_ref[...] = vec_own[k] + vec_got[k]
+
+    beside = line + 2 * (line % 2) - 1
+    lowest = jnp.where(line % 2 == 0, beside, -1)
+    highest = jnp.where(line % 2 == 1, beside, lines)
+    greet(lines, hops + far, lowest, highest, lambda l: device(pair, l, mid, core))
+
+    def far_first(function):
+        def step(k, carry):
+            distance = lines - 1 - k
+
+            @pl.when(line + distance < lines)
+            def _():
+                function(line + distance)
+
+            @pl.when((line - distance >= 0) & (distance > 0))
+            def _():
+                function(line - distance)
+
+            return carry
+
+        lax.fori_loop(0, lines, step, 0)
+
+    def start_sibling(l, s, t):
+        to_sibling(l, s, t).start()
+
+    sib_second, sib_third = at_third, at_second
+    for s, t in ((1, 1), (0, 1), (1, 0), (0, 0)):
+        s_at = sib_second + s * (1 - 2 * sib_second)
+        t_at = sib_third + t * (1 - 2 * sib_third)
+        far_first(lambda l, s_at=s_at, t_at=t_at: start_sibling(l, s_at, t_at))
+        s_own = at_second + s * (1 - 2 * at_second)
+        t_own = at_third + t * (1 - 2 * at_third)
+        far_first(lambda l, s_own=s_own, t_own=t_own: load(l, s_own, t_own).start())
+    vec_own[0] = vec_in[...]
+    vec_step(0).start()
+
+    def both_cores(l, s, t):
+        load(l, s, t).wait()
+        to_sibling(l, s, t).wait_recv()
+        index = spot(l, s, t)
+        return mine[index].astype(F32) + from_sib[index].astype(F32)
+
+    def send_third(l, s):
+        mine[spot(l, s, 1 - at_third)] = both_cores(l, s, 1 - at_third).astype(BF16)
+        to_third(l, s).start()
+
+    far_first(lambda l: send_third(l, 1 - at_second))
+    far_first(lambda l: send_third(l, at_second))
+    vec_next(0)
+
+    def with_third(l, s):
+        total = both_cores(l, s, at_third)
+        to_third(l, s).wait_recv()
+        return total + from_third[l * 2 + s].astype(F32)
+
+    def send_second(l):
+        mine[spot(l, 1 - at_second, at_third)] = with_third(l, 1 - at_second).astype(BF16)
+        to_second(l).start()
+
+    far_first(send_second)
+    vec_next(1)
+
+    def with_second(l):
+        total = with_third(l, at_second)
+        to_second(l).wait_recv()
+        return total + from_second[l].astype(F32)
+
+    def send_line(k, carry):
+        distance = lines - 1 - k
+        above = line + distance
+        below = line - distance
+
+        @pl.when(above < lines)
+        def _():
+            total = with_second(above)
+            index = spot(above, at_second, at_third)
+            mine[index] = total.astype(BF16)
+
+            @pl.when(line > 0)
+            def _():
+                to_upper(above).wait_recv()
+                mine[index] = (total + from_lower[above].astype(F32)).astype(BF16)
+
+            to_upper(above).start()
+
+        @pl.when(below >= 0)
+        def _():
+            total = with_second(below)
+            index = spot(below, at_second, at_third)
+            mine[index] = total.astype(BF16)
+
+            @pl.when(line < lines - 1)
+            def _():
+                to_lower(below).wait_recv()
+                mine[index] = (total + from_upper[below].astype(F32)).astype(BF16)
+
+            to_lower(below).start()
+
+        return carry
+
+    lax.fori_loop(0, lines - 1, send_line, 0)
+    vec_next(2)
+    sum_ref[...] = with_second(line)
+
+    @pl.when(line > 0)
+    def _():
+        to_upper(line).wait_recv()
+        sum_ref[...] += from_lower[line].astype(F32)
+
+    @pl.when(line < lines - 1)
+    def _():
+        to_lower(line).wait_recv()
+        sum_ref[...] += from_upper[line].astype(F32)
+
+    total = jnp.where(owned_ref[...] > 0, sum_ref[...], 0.0)
+    sum_ref[...] = total
+    square = jnp.sum((total * total).reshape(count * BLOCK // 8, 8, BLOCK), axis=0)
+    sq_own[0] = square
+
+    def sq_step(k):
+        to = (hops + far)[k]
+        return copy(sq_own.at[k], sq_got.at[k], sq_send.at[k], sq_recv.at[k], to)
+
+    sq_step(0).start()
+    for k in range(3 + steps):
+        if k > 2:
+            vec_next(k)
+        sq_step(k).wait_recv()
+        if k < 2 + steps:
+            sq_own[k + 1] = sq_own[k] + sq_got[k]
+            sq_step(k + 1).start()
+        else:
+            square_ref[...] = sq_own[k] + sq_got[k]
+
+    def finish(l, carry):
+        for s in range(2):
+            for t in range(2):
+                to_sibling(l, s, t).wait_send()
+            to_third(l, s).wait_send()
+        to_second(l).wait_send()
+
+        @pl.when((l > line) & (line < lines - 1))
+        def _():
+            to_upper(l).wait_send()
+
+        @pl.when((l < line) & (line > 0))
+        def _():
+            to_lower(l).wait_send()
+
+        return carry
+
+    lax.fori_loop(0, lines, finish, 0)
+    for k in range(3 + steps):
+        vec_step(k).wait_send()
+        sq_step(k).wait_send()
+
+
+def sum_by_slot(grads, vec, owned):
+    lines = lax.axis_size("dp") // 4
+    count = grads.shape[0] // (8 * lines)
+    steps = 3 + lines.bit_length() - 1
+    dma = pltpu.SemaphoreType.DMA
+    vmem = pl.BlockSpec(memory_space=pltpu.VMEM)
+    shard = (count, BLOCK, BLOCK)
+    owned = jnp.broadcast_to(owned.astype(F32)[:, None, None], (count, 1, BLOCK))
+    return pl.pallas_call(
+        partial(sum_kernel, lines),
+        out_shape=(
+            jax.ShapeDtypeStruct(shard, F32),
+            jax.ShapeDtypeStruct(vec.shape, F32),
+            jax.ShapeDtypeStruct((8, BLOCK), F32),
+        ),
+        in_specs=[pl.BlockSpec(memory_space=ANY), vmem, vmem],
+        out_specs=(vmem, vmem, vmem),
+        scratch_shapes=[
+            pltpu.VMEM((4 * lines,) + shard, BF16),
+            pltpu.VMEM((4 * lines,) + shard, BF16),
+            pltpu.VMEM((2 * lines,) + shard, BF16),
+            pltpu.VMEM((lines,) + shard, BF16),
+            pltpu.VMEM((lines,) + shard, BF16),
+            pltpu.VMEM((lines,) + shard, BF16),
+            pltpu.VMEM((steps,) + vec.shape, F32),
+            pltpu.VMEM((steps,) + vec.shape, F32),
+            pltpu.VMEM((steps, 8, BLOCK), F32),
+            pltpu.VMEM((steps, 8, BLOCK), F32),
+            dma((4 * lines,)),
+            dma((4 * lines,)),
+            dma((2 * lines,)),
+            dma((lines,)),
+            dma((lines,)),
+            dma((lines,)),
+            dma((4 * lines,)),
+            dma((2 * lines,)),
+            dma((lines,)),
+            dma((lines,)),
+            dma((lines,)),
+            dma((steps,)),
+            dma((steps,)),
+            dma((steps,)),
+            dma((steps,)),
+        ],
+        compiler_params=pltpu.CompilerParams(collective_id=1, has_side_effects=True, vmem_limit_bytes=48 * 1024 * 1024),
+        cost_estimate=pl.CostEstimate(flops=0, bytes_accessed=2 * grads.size * 2, transcendentals=0),
+    )(grads, vec, owned)
 
 
 def sigma_of(levels):
@@ -765,28 +1264,20 @@
     vec_second,
 ):
     slot_count = blocks.shape[0]
-    whole = lax.all_gather(blocks.astype(BF16), ("pair", "dp"), axis=0, tiled=True)
+    whole = gather_blocks(blocks)
     ready = prepare(
         big_images, big_noise, small_images, small_noise, big_level, small_level, small_mask, vectors, lax.axis_index("pair")
     )
-    grads, gvec, gin, ghead, loss = network_grads(owner_map, *ready, whole)
-    summed = lax.psum_scatter(grads.reshape(grads.shape[0], -1), ("pair", "dp"), scatter_dimension=0, tiled=True)
+    grads, vec_part = network_grads(owner_map, *ready, whole)
     slot_ids = lax.axis_index(("pair", "dp")) * slot_count + jnp.arange(slot_count, dtype=jnp.int32)
     owned = jnp.any(slot_ids[:, None] == owner_map[None, :], axis=1)
-    mine = jnp.where(owned[:, None], summed.astype(F32), 0.0)
-    vec_part = jnp.concatenate(
-        [
-            gin[0:72].reshape(9, 8, CH)[:, 0:3].reshape(27, CH),
-            gin[72:73],
-            gvec[28:47],
-            ghead[0:72].reshape(9, 8, CH)[:, 0:3].reshape(27, CH),
-        ],
-        axis=0,
-    )
-    vec_total, loss_total, square = lax.psum((vec_part, loss[0, 0], jnp.sum(mine * mine)), ("pair", "dp"))
-    grad_norm = jnp.sqrt(square + jnp.sum(vec_total * vec_total))
+    mine, vec_sum, square = sum_by_slot(grads, vec_part, owned)
+    count = vectors.shape[0]
+    vec_total = vec_sum[:count]
+    loss_total = vec_sum[count, 0]
+    grad_norm = jnp.sqrt(jnp.sum(square) + jnp.sum(vec_total * vec_total))
     factor = jnp.minimum(1.0, CLIP / (grad_norm + 1e-06))
-    slot_grad = mine.reshape(blocks.shape) * factor
+    slot_grad = mine * factor
     new_blocks, new_moments, new_left, new_right = shampoo(
         slot_grad, blocks, moments, left_stats, right_stats, left_roots, right_roots
     )

time: 592 us -> 254 us (0.43)
  waiting for transfers between devices: 179 us -> 0 us
  blocking collectives: 135 us -> 0 us
  Pallas kernels: 126 us -> 224 us
  starting transfers between devices: 60.5 us -> 0 us
  local copies, waits for them, and re-layouts: 50 us -> 13.1 us
  between operations: 17.1 us -> 3.65 us
  other arithmetic: 12.8 us -> 6.22 us
    psum x1 -> x0, waiting for transfers between devices: 113 us -> none  [local(): lax.psum((vec_part, loss[0, 0], jnp.sum(mine * mine)), ('pair', 'dp'))]
    pallas_call x0 -> x2, Pallas kernels: none -> 98.1 us  [the longest x1 61.1 us: sum_by_slot(): pl.pallas_call(partial(sum_kernel, lines), out_shape=(jax.ShapeDtypeStruc...]
    unnamed x1 -> x0, blocking collectives: 92.5 us -> none
    all_gather x1 -> x0, waiting for transfers between devices: 60.8 us -> none  [local(): lax.all_gather(blocks.astype(BF16), ('pair', 'dp'), axis=0, tiled=True)]
    unnamed x8 -> x0, starting transfers between devices: 60.5 us -> none
    psum x1 -> x0, blocking collectives: 42.6 us -> none  [local(): lax.psum((vec_part, loss[0, 0], jnp.sum(mine * mine)), ('pair', 'dp'))]
    unnamed x33 -> x28, local copies, waits for them, and re-layouts: 36.7 us -> 2.06 us
  transfers between devices with their start and end apart: 10 -> 0, of which waited for: 3 -> 0; matrix products, arithmetic and copies ran while one was open for 3% -> 0% of each run, Pallas kernels for 0% -> 0%
where the time goes in v2:
time: 254 us; the launch traced here: 251 us
  Pallas kernels  224 us (88%)
  local copies, waits for them, and re-layouts  13.1 us (5%)
  other arithmetic  6.22 us (2%)
  matrix products  4.78 us (2%)
  between operations  3.65 us (1%)
    pallas_call x1, Pallas kernels, network_grads(): pl.pallas_call(net_kernel, out_shape=(jax.ShapeDtypeStruct((slots, BLOCK,...  126 us
    pallas_call x1, Pallas kernels, sum_by_slot(): pl.pallas_call(partial(sum_kernel, lines), out_shape=(jax.ShapeDtypeStruc...  61.1 us
    pallas_call x1, Pallas kernels, gather_blocks(): pl.pallas_call(partial(gather_kernel, lines), out_shape=jax.ShapeDtypeStr...  37.1 us

profile of v2, /device:TPU:0, one launch (start us, length us, event | category | flops | bytes accessed | tf_op | source)
XLA Modules:
  0.0 251.4 jit_solution(2356103833464723923)
XLA Ops:
  0.6 0.0 copy-start
  0.7 0.0 copy-start.3
  0.7 0.8 dynamic_slice.21
  1.5 1.2 dynamic_slice.22
  2.7 0.7 pad_add_fusion
  3.5 0.1 copy.48
  3.6 0.1 reshape.227
  3.6 0.1 log_multiply_fusion
  3.7 0.1 subtract_divide_fusion
  3.8 0.1 select_maximum_fusion
  3.9 0.6 reshape.228.scal_ref
  4.5 0.1 reshape.236
  4.6 0.1 fusion.10
  4.7 0.6 fusion.9.emb_ref
  5.3 0.8 constant_dynamic-slice_fusion.3
  6.2 0.6 pad.40.big_ref
  6.8 0.6 pad.41.big_noise_ref
  7.5 0.7 constant_dynamic-slice_fusion.1
  8.2 0.6 pad.42.small_ref
  8.8 0.6 pad.43.small_noise_ref
  9.4 0.7 fusion.13
  10.1 0.6 broadcast_in_dim.9.mask_ref
  10.7 0.8 fusion.15
  11.5 0.1 pad.50.clone
  11.6 0.7 slice.24
  12.3 0.7 maximum_maximum_fusion.vin_ref
  13.0 0.6 pad.47.head_ref
  13.7 37.1 %shard_map.232.whole_ref = bf16[192,128,128]{2,1,0:T(8,128)(2,1)} custom-call(f32[6,128,128]{2,1,0:T(8,128)} %blocks_ref.1), custom_call_target="tpu_custom_call" | custom-call | bytes 12582912 | tf_op jit(solution)/shard_map/pallas_call | solution.py:854
  50.8 0.0 copy-done.3
  50.8 0.6 pad.44.vec_ref
  51.4 0.0 copy-start.10
  51.4 0.0 copy-start.8
  51.4 0.0 copy-start.9
  51.4 0.0 copy-start.5
  51.4 0.0 copy-start.6
  51.4 0.0 copy-start.4
  51.4 0.0 copy-start.7
  51.5 125.5 %shard_map.233 = (bf16[192,128,128]{2,1,0:T(8,128)(2,1)}, f32[80,256]{1,0:T(8,128)}) custom-call(s32[176]{0:T(256)} %owner_ref.1, f32[48]{0:T(128)} %reshape.228.scal_ref, bf16[16,256]{1,0:T(8,128)(2,1)} %fusion.9.emb_ref, f32[2,8,1024]{2,1,0:T(8,128)} %pad.40.big_ref, f32[2,8,1024]{2,1,0:T(8,128)} %pad.41.big_noise_ref, f32[1,8,256]{2,1,0:T(8,128)} %pad.42.small_ref, ...), custom_call_target="tpu_custom_call" | custom-call | flops 57000001536 | bytes 20000000 | tf_op jit(solution)/shard_map/pallas_call | solution.py:632
  177.0 0.0 copy-done.10
  177.0 0.2 compare_reduce_fusion
  177.2 0.1 broadcast_in_dim.11.owned_ref
  177.3 0.9 copy-done.1
  178.2 0.0 copy-start.2
  178.2 61.1 %shard_map.234 = (f32[6,128,128]{2,1,0:T(8,128)S(1)}, f32[80,256]{1,0:T(8,128)S(1)}, f32[8,128]{1,0:T(8,128)S(1)}) custom-call(bf16[192,128,128]{2,1,0:T(8,128)(2,1)} %get-tuple-element.14.grads_ref, f32[80,256]{1,0:T(8,128)S(1)} %copy-done.1, f32[6,1,128]{2,1,0:T(1,128)S(1)} %broadcast_in_dim.11.owned_ref), custom_call_target="tpu_custom_call" | custom-call | bytes 12582912 | tf_op jit(solution)/shard_map/pallas_call | solution.py:1133
  239.3 0.6 multiply_reduce_fusion.1
  239.9 0.6 reduce_sum.27
  241.9 0.0 copy-done.8
  241.9 0.0 copy-done.9
  241.9 0.7 multiply_subtract_fusion.1
  242.6 0.0 copy-done.5
  242.6 1.7 fusion
  244.3 0.0 copy-done.6
  244.3 1.6 fusion.1
  245.8 0.0 copy-done.4
  245.9 0.2 copy.53
  246.0 0.1 bitcast_add_fusion
  246.1 0.0 copy-done.7
  246.1 0.9 fusion.16
  247.0 0.0 copy-done
  247.1 0.6 multiply_reduce_fusion
  247.7 0.0 copy-done.2
  247.7 0.9 multiply_subtract_fusion
  248.6 0.9 copy.56
  249.5 0.5 slice.26
  (16 shorter events, 0.1 us)
Async XLA Ops:
  0.6 246.4 %copy-start = (f32[6,128,128]{2,1,0:T(8,128)S(1)}, f32[6,128,128]{2,1,0:T(8,128)}, u32[]{:S(2)}) copy-start(f32[6,128,128]{2,1,0:T(8,128)} %param.30) | copy-start | bytes 1179652
  0.7 50.1 %copy-start.3 = (f32[74,256]{1,0:T(8,128)S(1)}, f32[74,256]{1,0:T(8,128)}, u32[]{:S(2)}) copy-start(f32[74,256]{1,0:T(8,128)} %param.31) | copy-start | bytes 227332
  51.4 125.6 %copy-start.10 = (s32[176]{0:T(256)S(1)}, s32[176]{0:T(256)}, u32[]{:S(2)}) copy-start(s32[176]{0:T(256)} %owner_ref.1) | copy-start | bytes 2116
  51.4 190.5 %copy-start.8 = (f32[74,256]{1,0:T(8,128)S(1)}, f32[74,256]{1,0:T(8,128)}, u32[]{:S(2)}) copy-start(f32[74,256]{1,0:T(8,128)} %param.32) | copy-start | bytes 227332
  51.4 190.5 %copy-start.9 = (f32[74,256]{1,0:T(8,128)S(1)}, f32[74,256]{1,0:T(8,128)}, u32[]{:S(2)}) copy-start(f32[74,256]{1,0:T(8,128)} %param.33) | copy-start | bytes 227332
  51.4 191.2 %copy-start.5 = (f32[6,128,128]{2,1,0:T(8,128)S(1)}, f32[6,128,128]{2,1,0:T(8,128)}, u32[]{:S(2)}) copy-start(f32[6,128,128]{2,1,0:T(8,128)} %param.28) | copy-start | bytes 1179652
  51.4 192.9 %copy-start.6 = (f32[6,128,128]{2,1,0:T(8,128)S(1)}, f32[6,128,128]{2,1,0:T(8,128)}, u32[]{:S(2)}) copy-start(f32[6,128,128]{2,1,0:T(8,128)} %param.27) | copy-start | bytes 1179652
  51.4 194.4 %copy-start.4 = (f32[6,128,128]{2,1,0:T(8,128)S(1)}, f32[6,128,128]{2,1,0:T(8,128)}, u32[]{:S(2)}) copy-start(f32[6,128,128]{2,1,0:T(8,128)} %param.26) | copy-start | bytes 1179652
  51.4 194.6 %copy-start.7 = (f32[6,128,128]{2,1,0:T(8,128)S(1)}, f32[6,128,128]{2,1,0:T(8,128)}, u32[]{:S(2)}) copy-start(f32[6,128,128]{2,1,0:T(8,128)} %param.29) | copy-start | bytes 1179652
  177.3 0.9 copy-start.1
  178.2 69.5 %copy-start.2 = (f32[6,128,128]{2,1,0:T(8,128)S(1)}, f32[6,128,128]{2,1,0:T(8,128)}, u32[]{:S(2)}) copy-start(f32[6,128,128]{2,1,0:T(8,128)} %blocks_ref.1) | copy-start | bytes 1179652
